TPU v7x, 32 devices: a whole 2x2x4 slice. The times are simulated.
32 devices in a mesh: gx: 4 (over y, x), gy: 4 (over z), gz: 2 (over core).
Axes of the slice: x: 2, y: 2, z: 4, core: 2. Of those that a mesh axis runs over, the one named last changes fastest.
Arguments:
- velocity: float32 [3, 8, 4, 8, 512], P(None, 'gx', 'gy', 'gz'), may hold values from -4 to 4
- reaction: float32 [8, 4, 8, 512], P('gx', 'gy', 'gz'), may hold values from 10 to 100
Outputs:
- velocity_out: float32 [3, 8, 4, 8, 512], P(None, 'gx', 'gy', 'gz')
- pressure: float32 [8, 4, 8, 512], P('gx', 'gy', 'gz')
- residual: float32 [8, 4, 8, 512], P('gx', 'gy', 'gz')
All inputs are finite; a program needn't handle non-finite values.
Results may differ from a plain program's by a relative error of at most 0.007.
Values sent between devices are 32-bit elements; how exact they have to be, the bound alone decides.
No kernel may reach another device: no remote copies, remote signals or barrier semaphores. Data moves between devices by JAX's collectives and lax.ppermute only.
A program may use at most 64 MiB of HBM per device.

v0:
```python
import functools

import jax
import jax.numpy as jnp
import numpy as np
from jax import lax
from jax.experimental import pallas as pl
from jax.experimental.pallas import tpu as pltpu
from jax.sharding import PartitionSpec as P

SUBSTEPS = 2
ITERS = 4
step_size = 0.02

F32 = jnp.float32
BF16 = jnp.bfloat16


def legendre_seven(points):
    earlier = points * 0.0 + 1.0
    current = points
    for degree in range(1, 7):
        earlier, current = (
            current,
            ((2 * degree + 1) * points * current - degree * earlier) / (degree + 1),
        )
    return current


def host_tables():
    half = np.array([0.20929921790247888, 0.5917001814331423, 0.8717401485096066, 1.0])
    points = np.concatenate([-half[::-1], half])
    legendre = legendre_seven(points)
    weights = 2.0 / (56.0 * legendre**2)
    spacing = points[:, None] - points[None, :] + np.eye(8)
    derivative = legendre[:, None] / legendre[None, :] / spacing * (1.0 - np.eye(8))
    derivative[0, 0] = -14.0
    derivative[7, 7] = 14.0
    return weights, derivative


def tables():
    weights, derivative = host_tables()
    return (jnp.asarray(weights, F32), jnp.asarray(derivative, F32))


def split_matrix(matrix):
    matrix = matrix.astype(np.float32)
    high = matrix.astype(jnp.bfloat16)
    low = (matrix - high.astype(np.float32)).astype(jnp.bfloat16)
    return np.concatenate([high, high, low], axis=1)


def split_parts(values):
    high = values.astype(BF16)
    return high, (values - high.astype(F32)).astype(BF16)


def roll_lanes(parts, shift):
    turned = [pltpu.roll(part, shift, 1) for part in parts]
    lane = lax.broadcasted_iota(jnp.int32, parts[0].shape, 1)
    return [jnp.where(lane < shift, turned[i - 1], turned[i]) for i in range(len(parts))]


def roll_lanes_back(parts, shift):
    turned = [pltpu.roll(part, 128 - shift, 1) for part in parts]
    lane = lax.broadcasted_iota(jnp.int32, parts[0].shape, 1)
    count = len(parts)
    return [
        jnp.where(lane < 128 - shift, turned[i], turned[(i + 1) % count]) for i in range(count)
    ]


class Lanes:
    def __init__(self, counts):
        self.strides = (counts[1] * counts[2], counts[2], 1)
        lane = lax.broadcasted_iota(jnp.int32, (1, 128), 1)
        place = {1: (lane // counts[2]) % counts[1], 2: lane % counts[2]}
        self.has_next = {d: place[d] < counts[d] - 1 for d in (1, 2)}
        self.has_prev = {d: place[d] > 0 for d in (1, 2)}

    def factors(self, direction, mode):
        n, p = self.has_next[direction], self.has_prev[direction]
        if mode == "sum":
            return None, None, jnp.where(n, 1.0, 0.0), jnp.where(p, 1.0, 0.0)
        alone = 1.0 if mode == "avg" else 0.0
        return (
            jnp.where(n, 0.5, alone),
            jnp.where(p, 0.5, alone),
            jnp.where(n, 0.5, 0.0),
            jnp.where(p, 0.5, 0.0),
        )


def settle(ref, slabs, lanes, mode, split=None):
    if 0 in slabs:
        lower, upper = slabs[0], slabs[7]
        stride = lanes.strides[0]
        new_upper = [a + b for a, b in zip(upper, roll_lanes_back(lower, stride))]
        new_lower = [a + b for a, b in zip(lower, roll_lanes(upper, stride))]
        if mode != "sum":
            new_upper = [0.5 * a for a in new_upper]
            new_lower = [0.5 * a for a in new_lower]
        slabs = {**slabs, 0: new_lower, 7: new_upper}

    def joined(lower, upper, direction):
        stride = lanes.strides[direction]
        own_up, own_low, from_next, from_prev = lanes.factors(direction, mode)
        following, previous = pltpu.roll(lower, 128 - stride, 1), pltpu.roll(upper, stride, 1)
        if mode == "sum":
            return lower + previous * from_prev, upper + following * from_next
        if mode == "wall":
            return (lower + previous) * from_prev, (upper + following) * from_next
        return lower * own_low + previous * from_prev, upper * own_up + following * from_next

    for a, parts in slabs.items():
        for h, part in enumerate(parts):
            lower, upper = joined(part[:8], part[56:], 1)
            ref[h, pl.ds(64 * a, 8), :] = lower
            ref[h, pl.ds(64 * a + 8, 48), :] = part[8:56]
            ref[h, pl.ds(64 * a + 56, 8), :] = upper
            first, last = pl.ds(64 * a, 8, stride=8), pl.ds(64 * a + 7, 8, stride=8)
            lower, upper = joined(ref[h, first, :], ref[h, last, :], 2)
            ref[h, first, :] = lower
            ref[h, last, :] = upper
        if split is not None:
            store_split(split, ref, a)


def store_split(split, ref, a):
    rows = pl.ds(64 * a, 64)
    values = jnp.concatenate([ref[h, rows, :] for h in range(ref.shape[0])], axis=1)
    split[0, rows, :], split[1, rows, :] = split_parts(values)


SLAB_ORDER = ((0, 7), (1,), (2,), (3,), (4,), (5,), (6,))


def column_kernel(*refs):
    blocks, outs = refs[:-2], refs[-2:]
    is_low = lax.axis_index("gz") == 0
    for j, block in enumerate(blocks):
        for k in range(block.shape[0]):
            low, high = block[k, 0, 0], block[k, 1, 0]
            straight = jnp.concatenate([low, high], axis=0)
            turned = jnp.concatenate([high, low], axis=0)
            outs[k // 2][j, k % 2] = jnp.where(is_low, straight, turned)


def pair_kernel(first, second, out):
    out[0] = first[...]
    out[1] = second[...]


SMALL = pltpu.CompilerParams(vmem_limit_bytes=1 << 20)


def paired(first, second):
    vmem = pl.BlockSpec(memory_space=pltpu.VMEM)
    return pl.pallas_call(
        pair_kernel,
        out_shape=jax.ShapeDtypeStruct((2,) + first.shape, F32),
        in_specs=[vmem] * 2,
        out_specs=vmem,
        compiler_params=SMALL,
    )(first, second)


def whole_kernel(devices, weights, derivative, *refs):
    (
        near, far, near_other, far_other, cross_ref, matrix_ref, pair_ref,
        vel_out, pre_out, res_out,
        u, v, xs, rm, w, dinv, z, r, y, s, p, x, flip, vel_own, pre_own, res_own, sems,
    ) = [refs[0:2], refs[2:4], refs[4:6], refs[6:8], *refs[8:]]
    my_y, my_z = lax.axis_index("gy"), lax.axis_index("gz")
    fields = u.shape[0]
    halves = range(u.shape[1])
    per_half = devices[0] // len(halves)
    lanes = Lanes((2 * devices[0], devices[1], 8))
    stiff_sum = np.sum(weights[:, None] * derivative * derivative, axis=0)
    slab_rows = [pl.ds(64 * a, 64) for a in range(8)]
    pair_rows = [[pl.ds(64 * a + 16 * j, 16) for a in range(8)] for j in range(4)]

    is_low = my_z == 0
    is_even = lax.axis_index("gx") % 2 == 0
    sublane = lax.broadcasted_iota(jnp.int32, (8, 128), 0)
    own_rows = (sublane < 4) == is_low
    entry = [my_y ^ j for j in range(devices[1])]

    def tile(near, far, k, ahead, at, cols):
        by_x = (near[0], 1) if k < 2 else (far[1], 0)
        diagonal = (far[k // 2], 1)
        if ahead == 0:
            ref, i = near[k // 2], 0
        elif ahead == 2:
            ref, i = (far[0], 0) if k < 2 else (near[1], 1)
        else:
            first, second = (by_x, diagonal) if ahead == 1 else (diagonal, by_x)
            first, second = (ref[i, at, k % 2, :, cols] for ref, i in (first, second))
            return jnp.where(is_even, first, second)
        return ref[i, at, k % 2, :, cols]

    def to_lanes(k, chunk):
        cols = pl.ds(128 * chunk, 128)
        parts = []
        for half in halves:
            tiles = []
            for i in range(per_half):
                first, second = [], []
                for at in entry:
                    here = tile(near, far, k, half * per_half + i, at, cols)
                    there = tile(near_other, far_other, k, half * per_half + i, at, cols)
                    first.append(jnp.where(own_rows, here, there))
                    second.append(pltpu.roll(jnp.where(own_rows, there, here), 4, 0))
                tiles += first + second
            parts.append(jnp.concatenate(tiles, axis=0).T)
        return parts

    def halves_of(parts, chunk):
        return {2 * chunk + i: [part[64 * i : 64 * i + 64] for part in parts] for i in range(2)}

    for k in range(fields):
        for chunks in ((0, 3), (1,), (2,)):
            slabs = {}
            for chunk in chunks:
                slabs.update(halves_of(to_lanes(k, chunk), chunk))
            settle(u.at[k], slabs, lanes, "avg", xs.at[k])

    for chunks in ((0, 3), (1,), (2,)):
        slabs = {}
        for chunk in chunks:
            for a, react in halves_of(to_lanes(fields, chunk), chunk).items():
                mass = cross_ref[pl.ds(0, 64), :] * float(weights[a])
                diag = cross_ref[pl.ds(0, 64), :] * float(stiff_sum[a])
                diag += cross_ref[pl.ds(64, 64), :] * float(weights[a])
                react = [part * mass for part in react]
                for h in halves:
                    rm[h, slab_rows[a], :] = react[h]
                slabs[a] = [part + diag for part in react]
        settle(dinv, slabs, lanes, "sum")

    up, low, _, _ = lanes.factors(2, "avg")
    share_z = jnp.where(sublane == 7, up, jnp.where(sublane == 0, low, 1.0))
    up, low, _, _ = lanes.factors(1, "avg")
    for b in range(8):
        share = share_z * (low if b == 0 else up) if b in (0, 7) else share_z
        for a in range(8):
            for h in halves:
                rows = pl.ds(64 * a + 8 * b, 8)
                inverse = 1.0 / dinv[h, rows, :]
                dinv[h, rows, :] = inverse
                w[h, rows, :] = inverse * (share * 0.5 if a in (0, 7) else share)

    def in_halves(g):
        return [g[:, 128 * h : 128 * (h + 1)] for h in halves]

    def product(row, count, k, a):
        high, low = xs[k, 0, slab_rows[a], :], xs[k, 1, slab_rows[a], :]
        parts = jnp.concatenate([high, low, high], axis=0)
        return in_halves(
            jnp.dot(matrix_ref[pl.ds(row, count), :], parts, preferred_element_type=F32)
        )

    def product_first(row, k, j):
        high, low = (
            jnp.concatenate([xs[k, i, pair_rows[j][a], :] for a in range(8)], axis=0)
            for i in range(2)
        )
        parts = jnp.concatenate([high, low, high], axis=0)
        g = in_halves(
            jnp.dot(pair_ref[pl.ds(row, 128), :], parts, preferred_element_type=F32)
        )
        return [[part[16 * a : 16 * a + 16] for part in g] for a in range(8)]

    now, after = u, v
    for _ in range(SUBSTEPS):
        for k in range(fields):
            for j in range(4):
                g = product_first(0, k, j)
                for a, rows in enumerate(pair_rows[j]):
                    for h in halves:
                        after[k, h, rows, :] = now[k, h, rows, :] - now[0, h, rows, :] * g[a][h]
            for group in SLAB_ORDER:
                slabs = {}
                for a in group:
                    g = product(0, 128, k, a)
                    slabs[a] = [
                        after[k, h, slab_rows[a], :]
                        - now[1, h, slab_rows[a], :] * g[h][:64]
                        - now[2, h, slab_rows[a], :] * g[h][64:]
                        for h in halves
                    ]
                settle(after.at[k], slabs, lanes, "wall", xs.at[k])
        now, after = after, now

    def own_block(source, own):
        flip[...] = source.T
        size = own.shape[2]
        for i in range(own.shape[0]):
            start = i * lanes.strides[0] + my_y * lanes.strides[1]
            block = flip[pl.ds(pl.multiple_of(start, 8), 8), :]
            own[i, 0] = jnp.where(is_low, block[:size], block[size:])

    for j in range(4):
        g = product_first(0, 0, j)
        for a, rows in enumerate(pair_rows[j]):
            for h in halves:
                r[h, rows, :] = g[a][h]
    for group in SLAB_ORDER:
        slabs = {}
        for a in group:
            second, third = product(0, 64, 1, a), product(64, 64, 2, a)
            mass = cross_ref[pl.ds(0, 64), :] * float(-weights[a] / step_size)
            slabs[a] = [
                mass * (r[h, slab_rows[a], :] + second[h] + third[h]) for h in halves
            ]
        settle(r, slabs, lanes, "sum")

    for k in range(fields):
        own_block(now[k, 0], vel_own.at[k])
    send_velocity = pltpu.make_async_copy(vel_own, vel_out, sems.at[0])
    send_velocity.start()

    def total(acc):
        return jnp.sum(jnp.sum(acc, axis=0, keepdims=True), axis=1, keepdims=True)

    def begin_sweep(update):
        acc = jnp.zeros((64, 128), F32)
        for a, rows in enumerate(slab_rows):
            for h in halves:
                res = r[h, rows, :]
                if update is not None:
                    alpha, beta = update
                    image = y[h, rows, :]
                    if beta is not None:
                        image = image + beta * s[h, rows, :]
                    s[h, rows, :] = image
                    res = res - alpha * image
                    r[h, rows, :] = res
                acc += res * res * w[h, rows, :]
                z[h, rows, :] = res * dinv[h, rows, :]
            store_split(xs.at[0], z, a)
        for j in range(4):
            g = product_first(128, 0, j)
            cross = cross_ref[pl.ds(16 * j, 16), :]
            for a, rows in enumerate(pair_rows[j]):
                for h in halves:
                    y[h, rows, :] = cross * g[a][h]
        return total(acc)

    gamma = begin_sweep(None)
    alpha = beta = None
    for sweep in range(ITERS):
        acc = jnp.zeros((64, 128), F32)
        for group in SLAB_ORDER:
            slabs = {}
            for a in group:
                g = product(128 + 64 * min(a, 7 - a), 64, 0, a)
                slabs[a] = []
                for h in halves:
                    here = z[h, slab_rows[a], :]
                    image = y[h, slab_rows[a], :] + g[h] + rm[h, slab_rows[a], :] * here
                    acc += image * here
                    slabs[a].append(image)
            settle(y, slabs, lanes, "sum")
        delta = total(acc)
        if sweep:
            beta = gamma / gamma_before
            alpha = gamma / (delta - beta * gamma / alpha)
        else:
            alpha = gamma / delta
        for rows in slab_rows:
            search = z[0, rows, :]
            if sweep:
                search = search + beta * p[rows, :]
            p[rows, :] = search
            x[rows, :] = x[rows, :] + alpha * search if sweep else alpha * search
        if sweep < ITERS - 1:
            gamma_before, gamma = gamma, begin_sweep((alpha, beta))
    for rows in slab_rows:
        r[0, rows, :] -= alpha * (y[0, rows, :] + beta * s[0, rows, :])

    own_block(x[...], pre_own)
    send_pressure = pltpu.make_async_copy(pre_own, pre_out, sems.at[1])
    send_pressure.start()
    own_block(r[0], res_own)
    send_residual = pltpu.make_async_copy(res_own, res_out, sems.at[2])
    send_residual.start()
    send_velocity.wait()
    send_pressure.wait()
    send_residual.wait()


def whole_body(devices, velocity, reaction):
    fields = velocity.shape[0]
    lanes = int(np.prod(devices)) * 8
    weights, derivative = host_tables()
    eye = np.eye(8)
    stiffness = derivative.T @ (weights[:, None] * derivative)
    stiff_sum = np.sum(weights[:, None] * derivative * derivative, axis=0)
    across = np.kron(stiffness, np.diag(weights)) + np.kron(np.diag(weights), stiffness)
    matrices = np.concatenate(
        [
            split_matrix(step_size * np.kron(derivative, eye)),
            split_matrix(step_size * np.kron(eye, derivative)),
        ]
        + [split_matrix(weights[a] * across) for a in range(4)]
    )
    along = [step_size * derivative, stiffness]
    pairs = np.concatenate([split_matrix(np.kron(m, np.eye(16))) for m in along])
    cross = np.outer(weights, weights).reshape(-1)
    sides = np.outer(stiff_sum, weights).reshape(-1) + np.outer(weights, stiff_sum).reshape(-1)
    cross = np.broadcast_to(np.concatenate([cross, sides])[:, None], (128, 128))

    vmem = pl.BlockSpec(memory_space=pltpu.VMEM)
    hbm = pl.BlockSpec(memory_space=pltpu.HBM)
    def swapped(block, axis, mask):
        count = lax.axis_size(axis)
        return lax.ppermute(block, axis, [(i, i ^ mask) for i in range(count)])

    block = jnp.concatenate([velocity, reaction[None]], axis=0)
    column = jax.ShapeDtypeStruct((devices[1], 2, 8, 512), F32)
    first, second = pl.pallas_call(
        column_kernel,
        out_shape=[column, column],
        in_specs=[vmem] * devices[1],
        out_specs=[vmem, vmem],
        compiler_params=SMALL,
    )(block, *(swapped(block, "gy", mask) for mask in range(1, devices[1])))
    near = [paired(first, swapped(first, "gx", 1)), paired(second, swapped(second, "gx", 2))]
    far = [swapped(near[0], "gx", 2), swapped(near[1], "gx", 1)]
    others = [swapped(pair, "gz", 1) for pair in (*near, *far)]

    field = pltpu.VMEM((lanes // 128, 512, 128), F32)
    three = pltpu.VMEM((fields, lanes // 128, 512, 128), F32)
    one_half = pltpu.VMEM((512, 128), F32)
    own = pltpu.VMEM(reaction.shape, F32)
    return pl.pallas_call(
        functools.partial(whole_kernel, devices, weights, derivative),
        out_shape=(
            jax.ShapeDtypeStruct(velocity.shape, F32),
            jax.ShapeDtypeStruct(reaction.shape, F32),
            jax.ShapeDtypeStruct(reaction.shape, F32),
        ),
        in_specs=[vmem] * 11,
        out_specs=(hbm, hbm, hbm),
        scratch_shapes=[three, three, pltpu.VMEM((fields, 2, 512, lanes), BF16)]
        + [field] * 7
        + [one_half] * 2
        + [
            pltpu.VMEM((128, 512), F32),
            pltpu.VMEM(velocity.shape, F32),
            own,
            own,
            pltpu.SemaphoreType.DMA((3,)),
        ],
        compiler_params=pltpu.CompilerParams(vmem_limit_bytes=40 << 20),
    )(
        *near, *far, *others, jnp.asarray(cross, F32), jnp.asarray(matrices), jnp.asarray(pairs),
    )


def extended(block, sides, width, periodic):
    for axis, dim in sides:
        count = lax.axis_size(axis)
        forward = [(i, i + 1) for i in range(count - 1)]
        if periodic:
            forward.append((count - 1, 0))
        backward = [(target, source) for source, target in forward]
        low = lax.ppermute(
            lax.slice_in_dim(block, block.shape[dim] - width, None, axis=dim), axis, forward
        )
        high = lax.ppermute(lax.slice_in_dim(block, 0, width, axis=dim), axis, backward)
        block = jnp.concatenate([low, block, high], axis=dim)
    return block


def derive(values, derivative, along_dim, transposed):
    layout = values.shape
    matrix = derivative.T if transposed else derivative
    blocks = values.reshape(-1, 8, 8, 8)
    patterns = ("aq,nqbc->nabc", "bq,naqc->nabc", "cq,nabq->nabc")
    result = jnp.einsum(patterns[along_dim], matrix, blocks, precision=lax.Precision.HIGHEST)
    return result.reshape(layout)


def place_face(values, target_axis, position, update):
    selector = tuple(
        (position if place == target_axis else slice(None) for place in range(values.ndim))
    )
    return values.at[selector].set(update)


def faces_along_x(sequence):
    return extended(sequence, (("gx", 0),), 1, True)


def faces_along_y(sequence):
    return extended(sequence, (("gy", 0),), 1, False)


def faces_along_z(sequence):
    return extended(sequence, (("gz", 0),), 1, False)


def join_faces(values, along_dim, exchanger):
    lower_face = jnp.moveaxis(jnp.take(values, 0, axis=4 + along_dim), 1 + along_dim, 0)
    upper_face = jnp.moveaxis(jnp.take(values, 7, axis=4 + along_dim), 1 + along_dim, 0)
    elements = lower_face.shape[0]
    face_shape = lower_face.shape
    sequence = jnp.stack([lower_face, upper_face], axis=1).reshape(2 * elements, -1)
    padded = exchanger(sequence)
    paired = padded.reshape(elements + 1, 2, -1)
    totals = paired[:, 0] + paired[:, 1]
    new_lower = jnp.moveaxis(totals[:-1].reshape(face_shape), 0, 1 + along_dim)
    new_upper = jnp.moveaxis(totals[1:].reshape(face_shape), 0, 1 + along_dim)
    values = place_face(values, 4 + along_dim, 0, new_lower)
    return place_face(values, 4 + along_dim, 7, new_upper)


def assemble(values):
    exchangers = (faces_along_x, faces_along_y, faces_along_z)
    dim_order = (0, 1, 2)
    for along_dim in dim_order:
        values = join_faces(values, along_dim, exchangers[along_dim])
    return values


def dim_factors(local_count, offset, total_count, bounded_by_walls):
    element_ids = offset + jnp.arange(local_count)
    node_ids = jnp.arange(8)
    at_end = (node_ids[None, :] == 0) | (node_ids[None, :] == 7)
    low_wall = (element_ids[:, None] == 0) & (node_ids[None, :] == 0)
    high_wall = (element_ids[:, None] == total_count - 1) & (node_ids[None, :] == 7)
    on_wall = (low_wall | high_wall) & bounded_by_walls
    shared = at_end & jnp.logical_not(on_wall)
    return (jnp.where(shared, 2.0, 1.0).astype(jnp.float32), on_wall.astype(jnp.float32))


def spread_body(velocity, reaction):
    weights, derivative = tables()
    count_x, count_y, count_z = (reaction.shape[0], reaction.shape[1], reaction.shape[2])
    speed = velocity.reshape(3, count_x, count_y, count_z, 8, 8, 8)
    react = reaction.reshape(1, count_x, count_y, count_z, 8, 8, 8)
    mass_matrix = weights[:, None, None] * weights[None, :, None] * weights[None, None, :]
    factor_x, wall_x = dim_factors(
        count_x, lax.axis_index("gx") * count_x, lax.axis_size("gx") * count_x, False
    )
    factor_y, wall_y = dim_factors(
        count_y, lax.axis_index("gy") * count_y, lax.axis_size("gy") * count_y, True
    )
    factor_z, wall_z = dim_factors(
        count_z, lax.axis_index("gz") * count_z, lax.axis_size("gz") * count_z, True
    )
    multiplicity = (
        factor_x[None, :, None, None, :, None, None]
        * factor_y[None, None, :, None, None, :, None]
        * factor_z[None, None, None, :, None, None, :]
    )
    interior = (1.0 - wall_y[None, None, :, None, None, :, None]) * (
        1.0 - wall_z[None, None, None, :, None, None, :]
    )
    stiff_sum = jnp.sum(weights[:, None] * derivative * derivative, axis=0)
    diag_local = (
        stiff_sum[:, None, None] * weights[None, :, None] * weights[None, None, :]
        + weights[:, None, None] * stiff_sum[None, :, None] * weights[None, None, :]
        + weights[:, None, None] * weights[None, :, None] * stiff_sum[None, None, :]
    )
    diag_terms = diag_local + react * mass_matrix
    speed = assemble(speed) / multiplicity
    diagonal = None
    for substep in range(SUBSTEPS):
        gradient_fields = [derive(speed, derivative, along_dim, False) for along_dim in range(3)]
        transport = (
            speed[0:1] * gradient_fields[0]
            + speed[1:2] * gradient_fields[1]
            + speed[2:3] * gradient_fields[2]
        )
        tendency = assemble(mass_matrix * transport) / (mass_matrix * multiplicity)
        speed = interior * (speed - step_size * tendency)
    spread = (
        derive(speed[0:1], derivative, 0, False)
        + derive(speed[1:2], derivative, 1, False)
        + derive(speed[2:3], derivative, 2, False)
    )
    source = -assemble(mass_matrix * spread)
    diagonal = assemble(diag_terms)

    def local_inner(first, second):
        return jnp.sum(first * second / multiplicity)

    def norm_weighted_mass(residual_vec, precond_vec):
        return lax.psum(local_inner(residual_vec, precond_vec), ("gx", "gy", "gz"))

    pressure = jnp.zeros_like(source)
    residual = source
    precond = residual / diagonal
    search = precond
    progress = norm_weighted_mass(residual, precond)
    for sweep_index in range(ITERS):
        local_sum = react * mass_matrix * search
        for apply_along_dim in range(3):
            local_sum = local_sum + derive(
                mass_matrix * derive(search, derivative, apply_along_dim, False),
                derivative,
                apply_along_dim,
                True,
            )
        applied = assemble(local_sum)
        step_length = progress / lax.psum(local_inner(search, applied), ("gx", "gy", "gz"))
        pressure = pressure + step_length * search
        residual = residual - step_length * applied
        precond = residual / diagonal
        progress_next = norm_weighted_mass(residual, precond)
        search = precond + progress_next / progress * search
        progress = progress_next
    return (
        speed.reshape(3, count_x, count_y, count_z, 512),
        pressure.reshape(count_x, count_y, count_z, 512),
        residual.reshape(count_x, count_y, count_z, 512),
    )


def solution(mesh):
    in_specs = (P(None, "gx", "gy", "gz", None), P("gx", "gy", "gz", None))
    out_specs = (
        P(None, "gx", "gy", "gz", None),
        P("gx", "gy", "gz", None),
        P("gx", "gy", "gz", None),
    )
    devices = tuple(mesh.shape[axis] for axis in ("gx", "gy", "gz"))

    def body(velocity, reaction):
        if devices == (4, 4, 2) and reaction.shape[:3] == (2, 1, 4):
            return whole_body(devices, velocity, reaction)
        return spread_body(velocity, reaction)

    return jax.shard_map(body, mesh=mesh, in_specs=in_specs, out_specs=out_specs, check_vma=False)
```

profile of v0, /device:TPU:0, one launch (start us, length us, event | category | flops | bytes accessed | tf_op | source)
XLA Modules:
  0.0 35.5 jit_solution(14457852572099886541)
XLA Ops:
  0.6 0.8 %pad_maximum_fusion.refs_0_ = f32[4,2,1,4,512]{4,3,2,1,0:T(4,128)S(1)} fusion(f32[1,2,1,4,512]{4,3,2,1,0:T(4,128)} %bitcast.1, f32[3,2,1,4,512]{4,3,2,1,0:T(4,128)} %param.5), kind=kLoop, calls=%fused_computation | loop fusion | flops 16384 | bytes 131072 | tf_op jit(solution)/shard_map/concatenate | solution.py:421
  1.5 5.1 %collective-permute-start.2 = (f32[4,2,1,4,512]{4,3,2,1,0:T(4,128)S(1)}, f32[4,2,1,4,512]{4,3,2,1,0:T(4,128)S(1)}, u32[]{:S(2)}, u32[]{:S(2)}) collective-permute-start(f32[4,2,1,4,512]{4,3,2,1,0:T(4,128)S(1)} %pad_maximum_fusion.refs_0_), channel_id=1, source_target_pairs={{0,6},{2,4},{4,2},{6,0},{1,7},{3,5},{5,3},{7,1},{8,14},{10,12},{12... | collective-permute-start | bytes 196616 | tf_op jit(solution)/shard_map/ppermute | solution.py:419
  6.6 0.0 collective-permute-start.1
  6.6 0.6 %collective-permute-start = (f32[4,2,1,4,512]{4,3,2,1,0:T(4,128)S(1)}, f32[4,2,1,4,512]{4,3,2,1,0:T(4,128)S(1)}, u32[]{:S(2)}, u32[]{:S(2)}) collective-permute-start(f32[4,2,1,4,512]{4,3,2,1,0:T(4,128)S(1)} %pad_maximum_fusion.refs_0_), channel_id=1, source_target_pairs={{0,2},{2,0},{4,6},{6,4},{1,3},{3,1},{5,7},{7,5},{8,10},{10,8},{12,... | collective-permute-start | bytes 196616 | tf_op jit(solution)/shard_map/ppermute | solution.py:419
  7.2 1.9 %collective-permute-done.2.refs_3_ = f32[4,2,1,4,512]{4,3,2,1,0:T(4,128)S(1)} collective-permute-done((f32[4,2,1,4,512]{4,3,2,1,0:T(4,128)S(1)}, f32[4,2,1,4,512]{4,3,2,1,0:T(4,128)S(1)}, u32[]{:S(2)}, u32[]{:S(2)}) %collective-permute-start.2) | collective-permute-done | bytes 65568 | tf_op jit(solution)/shard_map/ppermute | solution.py:419
  9.2 3.0 %collective-permute-done.1.refs_2_ = f32[4,2,1,4,512]{4,3,2,1,0:T(4,128)S(1)} collective-permute-done((f32[4,2,1,4,512]{4,3,2,1,0:T(4,128)S(1)}, f32[4,2,1,4,512]{4,3,2,1,0:T(4,128)S(1)}, u32[]{:S(2)}, u32[]{:S(2)}) %collective-permute-start.1) | collective-permute-done | bytes 65568 | tf_op jit(solution)/shard_map/ppermute | solution.py:419
  12.2 0.0 collective-permute-done.refs_1_
  12.2 1.6 %collective-permute-start.4 = (f32[4,2,8,512]{3,2,1,0:T(8,128)S(1)}, f32[4,2,8,512]{3,2,1,0:T(8,128)S(1)}, u32[]{:S(2)}, u32[]{:S(2)}) collective-permute-start(f32[4,2,8,512]{3,2,1,0:T(8,128)S(1)} %get-tuple-element.6.first), channel_id=1, source_target_pairs={{0,16},{8,24},{16,0},{24,8},{1,17},{9,25},{17,1},{25,9},{2,18},{10... | collective-permute-start | bytes 393224 | tf_op jit(solution)/shard_map/ppermute | solution.py:419
  13.8 1.5 %collective-permute-start.3 = (f32[4,2,8,512]{3,2,1,0:T(8,128)S(1)}, f32[4,2,8,512]{3,2,1,0:T(8,128)S(1)}, u32[]{:S(2)}, u32[]{:S(2)}) collective-permute-start(f32[4,2,8,512]{3,2,1,0:T(8,128)S(1)} %get-tuple-element.5.first), channel_id=1, source_target_pairs={{0,8},{8,0},{16,24},{24,16},{1,9},{9,1},{17,25},{25,17},{2,10},{10... | collective-permute-start | bytes 393224 | tf_op jit(solution)/shard_map/ppermute | solution.py:419
  15.3 2.1 %collective-permute-done.4.second = f32[4,2,8,512]{3,2,1,0:T(8,128)S(1)} collective-permute-done((f32[4,2,8,512]{3,2,1,0:T(8,128)S(1)}, f32[4,2,8,512]{3,2,1,0:T(8,128)S(1)}, u32[]{:S(2)}, u32[]{:S(2)}) %collective-permute-start.4) | collective-permute-done | bytes 131104 | tf_op jit(solution)/shard_map/ppermute | solution.py:419
  17.4 0.0 copy-start
  17.4 0.0 copy-start.1
  17.4 0.0 copy-start.2
  17.4 1.7 %collective-permute-start.6 = (f32[2,4,2,8,512]{4,3,2,1,0:T(8,128)S(1)}, f32[2,4,2,8,512]{4,3,2,1,0:T(8,128)S(1)}, u32[]{:S(2)}, u32[]{:S(2)}) collective-permute-start(f32[2,4,2,8,512]{4,3,2,1,0:T(8,128)S(1)} %shard_map.78.refs_1_), channel_id=1, source_target_pairs={{0,8},{8,0},{16,24},{24,16},{1,9},{9,1},{17,25},{25,17},{2,10},{10... | collective-permute-start | bytes 786440 | tf_op jit(solution)/shard_map/ppermute | solution.py:419
  19.2 0.0 collective-permute-done.3.second
  19.2 1.6 %collective-permute-start.5 = (f32[2,4,2,8,512]{4,3,2,1,0:T(8,128)S(1)}, f32[2,4,2,8,512]{4,3,2,1,0:T(8,128)S(1)}, u32[]{:S(2)}, u32[]{:S(2)}) collective-permute-start(f32[2,4,2,8,512]{4,3,2,1,0:T(8,128)S(1)} %shard_map.77.refs_0_), channel_id=1, source_target_pairs={{0,16},{8,24},{16,0},{24,8},{1,17},{9,25},{17,1},{25,9},{2,18},{10... | collective-permute-start | bytes 786440 | tf_op jit(solution)/shard_map/ppermute | solution.py:419
  20.8 0.0 collective-permute-start.8
  20.8 0.5 %collective-permute-start.7 = (f32[2,4,2,8,512]{4,3,2,1,0:T(8,128)S(1)}, f32[2,4,2,8,512]{4,3,2,1,0:T(8,128)S(1)}, u32[]{:S(2)}, u32[]{:S(2)}) collective-permute-start(f32[2,4,2,8,512]{4,3,2,1,0:T(8,128)S(1)} %shard_map.77.refs_0_), channel_id=1, source_target_pairs={{0,1},{1,0},{2,3},{3,2},{4,5},{5,4},{6,7},{7,6},{8,9},{9,8},{10,11... | collective-permute-start | bytes 786440 | tf_op jit(solution)/shard_map/ppermute | solution.py:419
  21.3 3.3 %collective-permute-done.6.refs_3_ = f32[2,4,2,8,512]{4,3,2,1,0:T(8,128)S(1)} collective-permute-done((f32[2,4,2,8,512]{4,3,2,1,0:T(8,128)S(1)}, f32[2,4,2,8,512]{4,3,2,1,0:T(8,128)S(1)}, u32[]{:S(2)}, u32[]{:S(2)}) %collective-permute-start.6) | collective-permute-done | bytes 262176 | tf_op jit(solution)/shard_map/ppermute | solution.py:419
  24.6 0.0 collective-permute-start.10
  24.6 1.5 %collective-permute-done.5.refs_2_ = f32[2,4,2,8,512]{4,3,2,1,0:T(8,128)S(1)} collective-permute-done((f32[2,4,2,8,512]{4,3,2,1,0:T(8,128)S(1)}, f32[2,4,2,8,512]{4,3,2,1,0:T(8,128)S(1)}, u32[]{:S(2)}, u32[]{:S(2)}) %collective-permute-start.5) | collective-permute-done | bytes 262176 | tf_op jit(solution)/shard_map/ppermute | solution.py:419
  26.2 0.0 collective-permute-start.9
  26.2 0.0 collective-permute-done.8.refs_5_
  26.2 0.0 collective-permute-done.7.refs_4_
  26.2 0.0 collective-permute-done.10.refs_7_
  26.2 1.5 %collective-permute-done.9.refs_6_ = f32[2,4,2,8,512]{4,3,2,1,0:T(8,128)S(1)} collective-permute-done((f32[2,4,2,8,512]{4,3,2,1,0:T(8,128)S(1)}, f32[2,4,2,8,512]{4,3,2,1,0:T(8,128)S(1)}, u32[]{:S(2)}, u32[]{:S(2)}) %collective-permute-start.9) | collective-permute-done | bytes 262176 | tf_op jit(solution)/shard_map/ppermute | solution.py:419
  27.7 0.0 copy-done
  27.7 0.0 copy-done.1
  27.7 0.0 copy-done.2
  27.7 7.8 %shard_map.79 = (f32[3,2,1,4,512]{4,3,2,1,0:T(4,128)}, f32[2,1,4,512]{3,2,1,0:T(4,128)}, f32[2,1,4,512]{3,2,1,0:T(4,128)}) custom-call(f32[2,4,2,8,512]{4,3,2,1,0:T(8,128)S(1)} %shard_map.77.refs_0_, f32[2,4,2,8,512]{4,3,2,1,0:T(8,128)S(1)} %shard_map.78.refs_1_, f32[2,4,2,8,512]{4,3,2,1,0:T(8,128)S(1)} %collective-permute-done.5.refs_2_, ...), custom_call_target="tpu_custom_call" | custom-call | tf_op jit(solution)/shard_map/pallas_call | solution.py:438
  (3 shorter events, 0.1 us)
Async XLA Ops:
  1.5 7.7 %collective-permute-start.2 = (f32[4,2,1,4,512]{4,3,2,1,0:T(4,128)S(1)}, f32[4,2,1,4,512]{4,3,2,1,0:T(4,128)S(1)}, u32[]{:S(2)}, u32[]{:S(2)}) collective-permute-start(f32[4,2,1,4,512]{4,3,2,1,0:T(4,128)S(1)} %pad_maximum_fusion.refs_0_), channel_id=1, source_target_pairs={{0,6},{2,4},{4,2},{6,0},{1,7},{3,5},{5,3},{7,1},{8,14},{10,12},{12... | collective-permute-start | bytes 196616 | tf_op jit(solution)/shard_map/ppermute | solution.py:419
  6.6 5.6 %collective-permute-start.1 = (f32[4,2,1,4,512]{4,3,2,1,0:T(4,128)S(1)}, f32[4,2,1,4,512]{4,3,2,1,0:T(4,128)S(1)}, u32[]{:S(2)}, u32[]{:S(2)}) collective-permute-start(f32[4,2,1,4,512]{4,3,2,1,0:T(4,128)S(1)} %pad_maximum_fusion.refs_0_), channel_id=1, source_target_pairs={{0,4},{2,6},{4,0},{6,2},{1,5},{3,7},{5,1},{7,3},{8,12},{10,14},{12... | collective-permute-start | bytes 196616 | tf_op jit(solution)/shard_map/ppermute | solution.py:419
  6.6 5.6 %collective-permute-start = (f32[4,2,1,4,512]{4,3,2,1,0:T(4,128)S(1)}, f32[4,2,1,4,512]{4,3,2,1,0:T(4,128)S(1)}, u32[]{:S(2)}, u32[]{:S(2)}) collective-permute-start(f32[4,2,1,4,512]{4,3,2,1,0:T(4,128)S(1)} %pad_maximum_fusion.refs_0_), channel_id=1, source_target_pairs={{0,2},{2,0},{4,6},{6,4},{1,3},{3,1},{5,7},{7,5},{8,10},{10,8},{12,... | collective-permute-start | bytes 196616 | tf_op jit(solution)/shard_map/ppermute | solution.py:419
  12.2 5.1 %collective-permute-start.4 = (f32[4,2,8,512]{3,2,1,0:T(8,128)S(1)}, f32[4,2,8,512]{3,2,1,0:T(8,128)S(1)}, u32[]{:S(2)}, u32[]{:S(2)}) collective-permute-start(f32[4,2,8,512]{3,2,1,0:T(8,128)S(1)} %get-tuple-element.6.first), channel_id=1, source_target_pairs={{0,16},{8,24},{16,0},{24,8},{1,17},{9,25},{17,1},{25,9},{2,18},{10... | collective-permute-start | bytes 393224 | tf_op jit(solution)/shard_map/ppermute | solution.py:419
  13.8 5.3 %collective-permute-start.3 = (f32[4,2,8,512]{3,2,1,0:T(8,128)S(1)}, f32[4,2,8,512]{3,2,1,0:T(8,128)S(1)}, u32[]{:S(2)}, u32[]{:S(2)}) collective-permute-start(f32[4,2,8,512]{3,2,1,0:T(8,128)S(1)} %get-tuple-element.5.first), channel_id=1, source_target_pairs={{0,8},{8,0},{16,24},{24,16},{1,9},{9,1},{17,25},{25,17},{2,10},{10... | collective-permute-start | bytes 393224 | tf_op jit(solution)/shard_map/ppermute | solution.py:419
  17.4 10.3 %copy-start = (bf16[256,384]{1,0:T(8,128)(2,1)S(1)}, bf16[256,384]{1,0:T(8,128)(2,1)}, u32[]{:S(2)}) copy-start(bf16[256,384]{1,0:T(8,128)(2,1)} %constant.8.clone.refs_10_) | copy-start | bytes 589828
  17.4 10.3 %copy-start.1 = (bf16[384,192]{1,0:T(8,128)(2,1)S(1)}, bf16[384,192]{1,0:T(8,128)(2,1)}, u32[]{:S(2)}) copy-start(bf16[384,192]{1,0:T(8,128)(2,1)} %constant.7.clone.refs_9_) | copy-start | bytes 442372
  17.4 10.3 %copy-start.2 = (f32[128,128]{1,0:T(8,128)S(1)}, f32[128,128]{1,0:T(8,128)}, u32[]{:S(2)}) copy-start(f32[128,128]{1,0:T(8,128)} %constant.6.clone.refs_8_) | copy-start | bytes 196612
  17.4 7.2 %collective-permute-start.6 = (f32[2,4,2,8,512]{4,3,2,1,0:T(8,128)S(1)}, f32[2,4,2,8,512]{4,3,2,1,0:T(8,128)S(1)}, u32[]{:S(2)}, u32[]{:S(2)}) collective-permute-start(f32[2,4,2,8,512]{4,3,2,1,0:T(8,128)S(1)} %shard_map.78.refs_1_), channel_id=1, source_target_pairs={{0,8},{8,0},{16,24},{24,16},{1,9},{9,1},{17,25},{25,17},{2,10},{10... | collective-permute-start | bytes 786440 | tf_op jit(solution)/shard_map/ppermute | solution.py:419
  19.2 7.0 %collective-permute-start.5 = (f32[2,4,2,8,512]{4,3,2,1,0:T(8,128)S(1)}, f32[2,4,2,8,512]{4,3,2,1,0:T(8,128)S(1)}, u32[]{:S(2)}, u32[]{:S(2)}) collective-permute-start(f32[2,4,2,8,512]{4,3,2,1,0:T(8,128)S(1)} %shard_map.77.refs_0_), channel_id=1, source_target_pairs={{0,16},{8,24},{16,0},{24,8},{1,17},{9,25},{17,1},{25,9},{2,18},{10... | collective-permute-start | bytes 786440 | tf_op jit(solution)/shard_map/ppermute | solution.py:419
  20.8 5.4 %collective-permute-start.8 = (f32[2,4,2,8,512]{4,3,2,1,0:T(8,128)S(1)}, f32[2,4,2,8,512]{4,3,2,1,0:T(8,128)S(1)}, u32[]{:S(2)}, u32[]{:S(2)}) collective-permute-start(f32[2,4,2,8,512]{4,3,2,1,0:T(8,128)S(1)} %shard_map.78.refs_1_), channel_id=1, source_target_pairs={{0,1},{1,0},{2,3},{3,2},{4,5},{5,4},{6,7},{7,6},{8,9},{9,8},{10,11... | collective-permute-start | bytes 786440 | tf_op jit(solution)/shard_map/ppermute | solution.py:419
  20.8 5.4 %collective-permute-start.7 = (f32[2,4,2,8,512]{4,3,2,1,0:T(8,128)S(1)}, f32[2,4,2,8,512]{4,3,2,1,0:T(8,128)S(1)}, u32[]{:S(2)}, u32[]{:S(2)}) collective-permute-start(f32[2,4,2,8,512]{4,3,2,1,0:T(8,128)S(1)} %shard_map.77.refs_0_), channel_id=1, source_target_pairs={{0,1},{1,0},{2,3},{3,2},{4,5},{5,4},{6,7},{7,6},{8,9},{9,8},{10,11... | collective-permute-start | bytes 786440 | tf_op jit(solution)/shard_map/ppermute | solution.py:419
  24.6 1.6 %collective-permute-start.10 = (f32[2,4,2,8,512]{4,3,2,1,0:T(8,128)S(1)}, f32[2,4,2,8,512]{4,3,2,1,0:T(8,128)S(1)}, u32[]{:S(2)}, u32[]{:S(2)}) collective-permute-start(f32[2,4,2,8,512]{4,3,2,1,0:T(8,128)S(1)} %collective-permute-done.6.refs_3_), channel_id=1, source_target_pairs={{0,1},{1,0},{2,3},{3,2},{4,5},{5,4},{6,7},{7,6},{8,9},{9,8},{10,11... | collective-permute-start | bytes 786440 | tf_op jit(solution)/shard_map/ppermute | solution.py:419
  26.2 1.5 %collective-permute-start.9 = (f32[2,4,2,8,512]{4,3,2,1,0:T(8,128)S(1)}, f32[2,4,2,8,512]{4,3,2,1,0:T(8,128)S(1)}, u32[]{:S(2)}, u32[]{:S(2)}) collective-permute-start(f32[2,4,2,8,512]{4,3,2,1,0:T(8,128)S(1)} %collective-permute-done.5.refs_2_), channel_id=1, source_target_pairs={{0,1},{1,0},{2,3},{3,2},{4,5},{5,4},{6,7},{7,6},{8,9},{9,8},{10,11... | collective-permute-start | bytes 786440 | tf_op jit(solution)/shard_map/ppermute | solution.py:419
where the time goes:
time: 35.7 us; the launch traced here: 35.5 us
  waiting for transfers between devices  13.4 us (38%)
  starting transfers between devices  12.7 us (36%)
  Pallas kernels  7.85 us (22%)
  other arithmetic  0.83 us (2%)
  between operations  0.7 us (2%)
    ppermute x11, waiting for transfers between devices, swapped(): return lax.ppermute(block, axis, [(i, i ^ mask) for i in range(count)])  13.4 us
    ppermute x11, starting transfers between devices, swapped(): return lax.ppermute(block, axis, [(i, i ^ mask) for i in range(count)])  12.7 us
    pallas_call x1, Pallas kernels, whole_body(): pl.pallas_call(functools.partial(whole_kernel, devices, weights, derivati...  7.76 us
    concatenate x1, other arithmetic, whole_body(): block = jnp.concatenate([velocity, reaction[None]], axis=0)  0.83 us
  transfers between devices with their start and end apart: 11, of which 6 were waited for; matrix products, arithmetic and copies ran while one was open for 0% of the time, Pallas kernels for 0%

commit v1 on v0

--- a/solution.py
+++ b/solution.py
@@ -345,7 +345,7 @@
             cross = cross_ref[pl.ds(16 * j, 16), :]
             for a, rows in enumerate(pair_rows[j]):
                 for h in halves:
-                    y[h, rows, :] = cross * g[a][h]
+                    y[h, rows, :] = cross * g[a][h] + rm[h, rows, :] * z[h, rows, :]
         return total(acc)
 
     gamma = begin_sweep(None)
@@ -359,7 +359,7 @@
                 slabs[a] = []
                 for h in halves:
                     here = z[h, slab_rows[a], :]
-                    image = y[h, slab_rows[a], :] + g[h] + rm[h, slab_rows[a], :] * here
+                    image = y[h, slab_rows[a], :] + g[h]
                     acc += image * here
                     slabs[a].append(image)
             settle(y, slabs, lanes, "sum")
@@ -427,8 +427,11 @@
         out_specs=[vmem, vmem],
         compiler_params=SMALL,
     )(block, *(swapped(block, "gy", mask) for mask in range(1, devices[1])))
-    near = [paired(first, swapped(first, "gx", 1)), paired(second, swapped(second, "gx", 2))]
-    far = [swapped(near[0], "gx", 2), swapped(near[1], "gx", 1)]
+    first_x, second_y = swapped(first, "gx", 1), swapped(second, "gx", 2)
+    first_y, second_x = swapped(first, "gx", 2), swapped(second, "gx", 1)
+    first_diagonal, second_diagonal = swapped(first_x, "gx", 2), swapped(second_y, "gx", 1)
+    near = [paired(first, first_x), paired(second, second_y)]
+    far = [paired(first_y, first_diagonal), paired(second_x, second_diagonal)]
     others = [swapped(pair, "gz", 1) for pair in (*near, *far)]
 
     field = pltpu.VMEM((lanes // 128, 512, 128), F32)

time: 35.7 us -> 35.5 us (level)
  waiting for transfers between devices: 13.4 us -> 12.6 us
  starting transfers between devices: 12.7 us -> 13.3 us
    ppermute x11 -> x13, waiting for transfers between devices: 13.4 us -> 12.6 us  [swapped(): return lax.ppermute(block, axis, [(i, i ^ mask) for i in range(count)])]
    ppermute x11 -> x13, starting transfers between devices: 12.7 us -> 13.3 us  [swapped(): return lax.ppermute(block, axis, [(i, i ^ mask) for i in range(count)])]
  transfers between devices with their start and end apart: 11 -> 13, of which waited for: 6 -> 7; matrix products, arithmetic and copies ran while one was open for 0% -> 0% of each run, Pallas kernels for 0% -> 0%
where the time goes in v1:
time: 35.5 us; the launch traced here: 35.3 us
  starting transfers between devices  13.3 us (37%)
  waiting for transfers between devices  12.6 us (35%)
  Pallas kernels  7.83 us (22%)
  other arithmetic  0.83 us (2%)
  between operations  0.75 us (2%)
    ppermute x13, starting transfers between devices, swapped(): return lax.ppermute(block, axis, [(i, i ^ mask) for i in range(count)])  13.3 us
    ppermute x13, waiting for transfers between devices, swapped(): return lax.ppermute(block, axis, [(i, i ^ mask) for i in range(count)])  12.6 us
    pallas_call x1, Pallas kernels, whole_body(): pl.pallas_call(functools.partial(whole_kernel, devices, weights, derivati...  7.71 us
    concatenate x1, other arithmetic, whole_body(): block = jnp.concatenate([velocity, reaction[None]], axis=0)  0.83 us
  transfers between devices with their start and end apart: 13, of which 7 were waited for; matrix products, arithmetic and copies ran while one was open for 0% of the time, Pallas kernels for 0%

profile of v1, /device:TPU:0, one launch (start us, length us, event | category | flops | bytes accessed | tf_op | source)
XLA Modules:
  0.0 35.3 jit_solution(47348333628106958)
XLA Ops:
  0.6 0.8 %pad_maximum_fusion.refs_0_ = f32[4,2,1,4,512]{4,3,2,1,0:T(4,128)S(1)} fusion(f32[1,2,1,4,512]{4,3,2,1,0:T(4,128)} %bitcast.1, f32[3,2,1,4,512]{4,3,2,1,0:T(4,128)} %param.5), kind=kLoop, calls=%fused_computation | loop fusion | flops 16384 | bytes 131072 | tf_op jit(solution)/shard_map/concatenate | solution.py:421
  1.5 5.1 %collective-permute-start.2 = (f32[4,2,1,4,512]{4,3,2,1,0:T(4,128)S(1)}, f32[4,2,1,4,512]{4,3,2,1,0:T(4,128)S(1)}, u32[]{:S(2)}, u32[]{:S(2)}) collective-permute-start(f32[4,2,1,4,512]{4,3,2,1,0:T(4,128)S(1)} %pad_maximum_fusion.refs_0_), channel_id=1, source_target_pairs={{0,6},{2,4},{4,2},{6,0},{1,7},{3,5},{5,3},{7,1},{8,14},{10,12},{12... | collective-permute-start | bytes 196616 | tf_op jit(solution)/shard_map/ppermute | solution.py:419
  6.6 0.0 collective-permute-start.1
  6.6 0.6 %collective-permute-start = (f32[4,2,1,4,512]{4,3,2,1,0:T(4,128)S(1)}, f32[4,2,1,4,512]{4,3,2,1,0:T(4,128)S(1)}, u32[]{:S(2)}, u32[]{:S(2)}) collective-permute-start(f32[4,2,1,4,512]{4,3,2,1,0:T(4,128)S(1)} %pad_maximum_fusion.refs_0_), channel_id=1, source_target_pairs={{0,2},{2,0},{4,6},{6,4},{1,3},{3,1},{5,7},{7,5},{8,10},{10,8},{12,... | collective-permute-start | bytes 196616 | tf_op jit(solution)/shard_map/ppermute | solution.py:419
  7.2 1.9 %collective-permute-done.2.refs_3_ = f32[4,2,1,4,512]{4,3,2,1,0:T(4,128)S(1)} collective-permute-done((f32[4,2,1,4,512]{4,3,2,1,0:T(4,128)S(1)}, f32[4,2,1,4,512]{4,3,2,1,0:T(4,128)S(1)}, u32[]{:S(2)}, u32[]{:S(2)}) %collective-permute-start.2) | collective-permute-done | bytes 65568 | tf_op jit(solution)/shard_map/ppermute | solution.py:419
  9.2 3.0 %collective-permute-done.1.refs_2_ = f32[4,2,1,4,512]{4,3,2,1,0:T(4,128)S(1)} collective-permute-done((f32[4,2,1,4,512]{4,3,2,1,0:T(4,128)S(1)}, f32[4,2,1,4,512]{4,3,2,1,0:T(4,128)S(1)}, u32[]{:S(2)}, u32[]{:S(2)}) %collective-permute-start.1) | collective-permute-done | bytes 65568 | tf_op jit(solution)/shard_map/ppermute | solution.py:419
  12.2 0.0 collective-permute-done.refs_1_
  12.2 1.6 %collective-permute-start.4 = (f32[4,2,8,512]{3,2,1,0:T(8,128)S(1)}, f32[4,2,8,512]{3,2,1,0:T(8,128)S(1)}, u32[]{:S(2)}, u32[]{:S(2)}) collective-permute-start(f32[4,2,8,512]{3,2,1,0:T(8,128)S(1)} %get-tuple-element.6.first), channel_id=1, source_target_pairs={{0,16},{8,24},{16,0},{24,8},{1,17},{9,25},{17,1},{25,9},{2,18},{10... | collective-permute-start | bytes 393224 | tf_op jit(solution)/shard_map/ppermute | solution.py:419
  13.8 1.5 %collective-permute-start.3 = (f32[4,2,8,512]{3,2,1,0:T(8,128)S(1)}, f32[4,2,8,512]{3,2,1,0:T(8,128)S(1)}, u32[]{:S(2)}, u32[]{:S(2)}) collective-permute-start(f32[4,2,8,512]{3,2,1,0:T(8,128)S(1)} %get-tuple-element.5.first), channel_id=1, source_target_pairs={{0,8},{8,0},{16,24},{24,16},{1,9},{9,1},{17,25},{25,17},{2,10},{10... | collective-permute-start | bytes 393224 | tf_op jit(solution)/shard_map/ppermute | solution.py:419
  15.3 0.5 %collective-permute-start.7 = (f32[4,2,8,512]{3,2,1,0:T(8,128)S(1)}, f32[4,2,8,512]{3,2,1,0:T(8,128)S(1)}, u32[]{:S(2)}, u32[]{:S(2)}) collective-permute-start(f32[4,2,8,512]{3,2,1,0:T(8,128)S(1)} %get-tuple-element.6.first), channel_id=1, source_target_pairs={{0,8},{8,0},{16,24},{24,16},{1,9},{9,1},{17,25},{25,17},{2,10},{10... | collective-permute-start | bytes 393224 | tf_op jit(solution)/shard_map/ppermute | solution.py:419
  15.9 1.5 %collective-permute-done.4.second = f32[4,2,8,512]{3,2,1,0:T(8,128)S(1)} collective-permute-done((f32[4,2,8,512]{3,2,1,0:T(8,128)S(1)}, f32[4,2,8,512]{3,2,1,0:T(8,128)S(1)}, u32[]{:S(2)}, u32[]{:S(2)}) %collective-permute-start.4) | collective-permute-done | bytes 131104 | tf_op jit(solution)/shard_map/ppermute | solution.py:419
  17.4 1.7 %collective-permute-start.8 = (f32[4,2,8,512]{3,2,1,0:T(8,128)S(1)}, f32[4,2,8,512]{3,2,1,0:T(8,128)S(1)}, u32[]{:S(2)}, u32[]{:S(2)}) collective-permute-start(f32[4,2,8,512]{3,2,1,0:T(8,128)S(1)} %collective-permute-done.4.second), channel_id=1, source_target_pairs={{0,8},{8,0},{16,24},{24,16},{1,9},{9,1},{17,25},{25,17},{2,10},{10... | collective-permute-start | bytes 393224 | tf_op jit(solution)/shard_map/ppermute | solution.py:419
  19.0 1.5 %collective-permute-start.5 = (f32[4,2,8,512]{3,2,1,0:T(8,128)S(1)}, f32[4,2,8,512]{3,2,1,0:T(8,128)S(1)}, u32[]{:S(2)}, u32[]{:S(2)}) collective-permute-start(f32[4,2,8,512]{3,2,1,0:T(8,128)S(1)} %get-tuple-element.5.first), channel_id=1, source_target_pairs={{0,16},{8,24},{16,0},{24,8},{1,17},{9,25},{17,1},{25,9},{2,18},{10... | collective-permute-start | bytes 393224 | tf_op jit(solution)/shard_map/ppermute | solution.py:419
  20.6 0.0 collective-permute-done.3.second
  20.6 0.5 %collective-permute-start.6 = (f32[4,2,8,512]{3,2,1,0:T(8,128)S(1)}, f32[4,2,8,512]{3,2,1,0:T(8,128)S(1)}, u32[]{:S(2)}, u32[]{:S(2)}) collective-permute-start(f32[4,2,8,512]{3,2,1,0:T(8,128)S(1)} %collective-permute-done.3.second), channel_id=1, source_target_pairs={{0,16},{8,24},{16,0},{24,8},{1,17},{9,25},{17,1},{25,9},{2,18},{10... | collective-permute-start | bytes 393224 | tf_op jit(solution)/shard_map/ppermute | solution.py:419
  21.1 0.1 collective-permute-start.10
  21.2 1.8 %collective-permute-done.7.first = f32[4,2,8,512]{3,2,1,0:T(8,128)S(1)} collective-permute-done((f32[4,2,8,512]{3,2,1,0:T(8,128)S(1)}, f32[4,2,8,512]{3,2,1,0:T(8,128)S(1)}, u32[]{:S(2)}, u32[]{:S(2)}) %collective-permute-start.7) | collective-permute-done | bytes 131104 | tf_op jit(solution)/shard_map/ppermute | solution.py:419
  23.0 0.0 collective-permute-start.9
  23.0 1.4 %collective-permute-done.8.second = f32[4,2,8,512]{3,2,1,0:T(8,128)S(1)} collective-permute-done((f32[4,2,8,512]{3,2,1,0:T(8,128)S(1)}, f32[4,2,8,512]{3,2,1,0:T(8,128)S(1)}, u32[]{:S(2)}, u32[]{:S(2)}) %collective-permute-start.8) | collective-permute-done | bytes 131104 | tf_op jit(solution)/shard_map/ppermute | solution.py:419
  24.4 0.0 copy-start
  24.4 0.0 copy-start.1
  24.5 0.0 copy-start.2
  24.5 0.1 collective-permute-start.12
  24.5 0.0 collective-permute-done.5.first
  24.6 1.4 %collective-permute-done.6.second = f32[4,2,8,512]{3,2,1,0:T(8,128)S(1)} collective-permute-done((f32[4,2,8,512]{3,2,1,0:T(8,128)S(1)}, f32[4,2,8,512]{3,2,1,0:T(8,128)S(1)}, u32[]{:S(2)}, u32[]{:S(2)}) %collective-permute-start.6) | collective-permute-done | bytes 131104 | tf_op jit(solution)/shard_map/ppermute | solution.py:419
  26.0 0.1 collective-permute-start.11
  26.1 0.0 collective-permute-done.10.refs_5_
  26.1 0.0 collective-permute-done.9.refs_4_
  26.1 0.0 collective-permute-done.12.refs_7_
  26.1 1.5 %collective-permute-done.11.refs_6_ = f32[2,4,2,8,512]{4,3,2,1,0:T(8,128)S(1)} collective-permute-done((f32[2,4,2,8,512]{4,3,2,1,0:T(8,128)S(1)}, f32[2,4,2,8,512]{4,3,2,1,0:T(8,128)S(1)}, u32[]{:S(2)}, u32[]{:S(2)}) %collective-permute-start.11) | collective-permute-done | bytes 262176 | tf_op jit(solution)/shard_map/ppermute | solution.py:419
  27.6 0.0 copy-done
  27.6 0.0 copy-done.1
  27.6 0.0 copy-done.2
  27.6 7.7 %shard_map.81 = (f32[3,2,1,4,512]{4,3,2,1,0:T(4,128)}, f32[2,1,4,512]{3,2,1,0:T(4,128)}, f32[2,1,4,512]{3,2,1,0:T(4,128)}) custom-call(f32[2,4,2,8,512]{4,3,2,1,0:T(8,128)S(1)} %shard_map.77.refs_0_, f32[2,4,2,8,512]{4,3,2,1,0:T(8,128)S(1)} %shard_map.78.refs_1_, f32[2,4,2,8,512]{4,3,2,1,0:T(8,128)S(1)} %shard_map.79.refs_2_, ...), custom_call_target="tpu_custom_call" | custom-call | tf_op jit(solution)/shard_map/pallas_call | solution.py:441
  (5 shorter events, 0.1 us)
Async XLA Ops:
  1.5 7.7 %collective-permute-start.2 = (f32[4,2,1,4,512]{4,3,2,1,0:T(4,128)S(1)}, f32[4,2,1,4,512]{4,3,2,1,0:T(4,128)S(1)}, u32[]{:S(2)}, u32[]{:S(2)}) collective-permute-start(f32[4,2,1,4,512]{4,3,2,1,0:T(4,128)S(1)} %pad_maximum_fusion.refs_0_), channel_id=1, source_target_pairs={{0,6},{2,4},{4,2},{6,0},{1,7},{3,5},{5,3},{7,1},{8,14},{10,12},{12... | collective-permute-start | bytes 196616 | tf_op jit(solution)/shard_map/ppermute | solution.py:419
  6.6 5.6 %collective-permute-start.1 = (f32[4,2,1,4,512]{4,3,2,1,0:T(4,128)S(1)}, f32[4,2,1,4,512]{4,3,2,1,0:T(4,128)S(1)}, u32[]{:S(2)}, u32[]{:S(2)}) collective-permute-start(f32[4,2,1,4,512]{4,3,2,1,0:T(4,128)S(1)} %pad_maximum_fusion.refs_0_), channel_id=1, source_target_pairs={{0,4},{2,6},{4,0},{6,2},{1,5},{3,7},{5,1},{7,3},{8,12},{10,14},{12... | collective-permute-start | bytes 196616 | tf_op jit(solution)/shard_map/ppermute | solution.py:419
  6.6 5.6 %collective-permute-start = (f32[4,2,1,4,512]{4,3,2,1,0:T(4,128)S(1)}, f32[4,2,1,4,512]{4,3,2,1,0:T(4,128)S(1)}, u32[]{:S(2)}, u32[]{:S(2)}) collective-permute-start(f32[4,2,1,4,512]{4,3,2,1,0:T(4,128)S(1)} %pad_maximum_fusion.refs_0_), channel_id=1, source_target_pairs={{0,2},{2,0},{4,6},{6,4},{1,3},{3,1},{5,7},{7,5},{8,10},{10,8},{12,... | collective-permute-start | bytes 196616 | tf_op jit(solution)/shard_map/ppermute | solution.py:419
  12.2 5.1 %collective-permute-start.4 = (f32[4,2,8,512]{3,2,1,0:T(8,128)S(1)}, f32[4,2,8,512]{3,2,1,0:T(8,128)S(1)}, u32[]{:S(2)}, u32[]{:S(2)}) collective-permute-start(f32[4,2,8,512]{3,2,1,0:T(8,128)S(1)} %get-tuple-element.6.first), channel_id=1, source_target_pairs={{0,16},{8,24},{16,0},{24,8},{1,17},{9,25},{17,1},{25,9},{2,18},{10... | collective-permute-start | bytes 393224 | tf_op jit(solution)/shard_map/ppermute | solution.py:419
  13.8 6.7 %collective-permute-start.3 = (f32[4,2,8,512]{3,2,1,0:T(8,128)S(1)}, f32[4,2,8,512]{3,2,1,0:T(8,128)S(1)}, u32[]{:S(2)}, u32[]{:S(2)}) collective-permute-start(f32[4,2,8,512]{3,2,1,0:T(8,128)S(1)} %get-tuple-element.5.first), channel_id=1, source_target_pairs={{0,8},{8,0},{16,24},{24,16},{1,9},{9,1},{17,25},{25,17},{2,10},{10... | collective-permute-start | bytes 393224 | tf_op jit(solution)/shard_map/ppermute | solution.py:419
  15.3 7.7 %collective-permute-start.7 = (f32[4,2,8,512]{3,2,1,0:T(8,128)S(1)}, f32[4,2,8,512]{3,2,1,0:T(8,128)S(1)}, u32[]{:S(2)}, u32[]{:S(2)}) collective-permute-start(f32[4,2,8,512]{3,2,1,0:T(8,128)S(1)} %get-tuple-element.6.first), channel_id=1, source_target_pairs={{0,8},{8,0},{16,24},{24,16},{1,9},{9,1},{17,25},{25,17},{2,10},{10... | collective-permute-start | bytes 393224 | tf_op jit(solution)/shard_map/ppermute | solution.py:419
  17.4 7.0 %collective-permute-start.8 = (f32[4,2,8,512]{3,2,1,0:T(8,128)S(1)}, f32[4,2,8,512]{3,2,1,0:T(8,128)S(1)}, u32[]{:S(2)}, u32[]{:S(2)}) collective-permute-start(f32[4,2,8,512]{3,2,1,0:T(8,128)S(1)} %collective-permute-done.4.second), channel_id=1, source_target_pairs={{0,8},{8,0},{16,24},{24,16},{1,9},{9,1},{17,25},{25,17},{2,10},{10... | collective-permute-start | bytes 393224 | tf_op jit(solution)/shard_map/ppermute | solution.py:419
  19.0 5.5 %collective-permute-start.5 = (f32[4,2,8,512]{3,2,1,0:T(8,128)S(1)}, f32[4,2,8,512]{3,2,1,0:T(8,128)S(1)}, u32[]{:S(2)}, u32[]{:S(2)}) collective-permute-start(f32[4,2,8,512]{3,2,1,0:T(8,128)S(1)} %get-tuple-element.5.first), channel_id=1, source_target_pairs={{0,16},{8,24},{16,0},{24,8},{1,17},{9,25},{17,1},{25,9},{2,18},{10... | collective-permute-start | bytes 393224 | tf_op jit(solution)/shard_map/ppermute | solution.py:419
  20.6 5.4 %collective-permute-start.6 = (f32[4,2,8,512]{3,2,1,0:T(8,128)S(1)}, f32[4,2,8,512]{3,2,1,0:T(8,128)S(1)}, u32[]{:S(2)}, u32[]{:S(2)}) collective-permute-start(f32[4,2,8,512]{3,2,1,0:T(8,128)S(1)} %collective-permute-done.3.second), channel_id=1, source_target_pairs={{0,16},{8,24},{16,0},{24,8},{1,17},{9,25},{17,1},{25,9},{2,18},{10... | collective-permute-start | bytes 393224 | tf_op jit(solution)/shard_map/ppermute | solution.py:419
  21.1 5.0 %collective-permute-start.10 = (f32[2,4,2,8,512]{4,3,2,1,0:T(8,128)S(1)}, f32[2,4,2,8,512]{4,3,2,1,0:T(8,128)S(1)}, u32[]{:S(2)}, u32[]{:S(2)}) collective-permute-start(f32[2,4,2,8,512]{4,3,2,1,0:T(8,128)S(1)} %shard_map.78.refs_1_), channel_id=1, source_target_pairs={{0,1},{1,0},{2,3},{3,2},{4,5},{5,4},{6,7},{7,6},{8,9},{9,8},{10,11... | collective-permute-start | bytes 786440 | tf_op jit(solution)/shard_map/ppermute | solution.py:419
  23.0 3.1 %collective-permute-start.9 = (f32[2,4,2,8,512]{4,3,2,1,0:T(8,128)S(1)}, f32[2,4,2,8,512]{4,3,2,1,0:T(8,128)S(1)}, u32[]{:S(2)}, u32[]{:S(2)}) collective-permute-start(f32[2,4,2,8,512]{4,3,2,1,0:T(8,128)S(1)} %shard_map.77.refs_0_), channel_id=1, source_target_pairs={{0,1},{1,0},{2,3},{3,2},{4,5},{5,4},{6,7},{7,6},{8,9},{9,8},{10,11... | collective-permute-start | bytes 786440 | tf_op jit(solution)/shard_map/ppermute | solution.py:419
  24.4 3.1 %copy-start = (bf16[256,384]{1,0:T(8,128)(2,1)S(1)}, bf16[256,384]{1,0:T(8,128)(2,1)}, u32[]{:S(2)}) copy-start(bf16[256,384]{1,0:T(8,128)(2,1)} %constant.8.clone.refs_10_) | copy-start | bytes 589828
  24.4 3.1 %copy-start.1 = (bf16[384,192]{1,0:T(8,128)(2,1)S(1)}, bf16[384,192]{1,0:T(8,128)(2,1)}, u32[]{:S(2)}) copy-start(bf16[384,192]{1,0:T(8,128)(2,1)} %constant.7.clone.refs_9_) | copy-start | bytes 442372
  24.5 3.1 %copy-start.2 = (f32[128,128]{1,0:T(8,128)S(1)}, f32[128,128]{1,0:T(8,128)}, u32[]{:S(2)}) copy-start(f32[128,128]{1,0:T(8,128)} %constant.6.clone.refs_8_) | copy-start | bytes 196612
  24.5 1.6 %collective-permute-start.12 = (f32[2,4,2,8,512]{4,3,2,1,0:T(8,128)S(1)}, f32[2,4,2,8,512]{4,3,2,1,0:T(8,128)S(1)}, u32[]{:S(2)}, u32[]{:S(2)}) collective-permute-start(f32[2,4,2,8,512]{4,3,2,1,0:T(8,128)S(1)} %shard_map.80.refs_3_), channel_id=1, source_target_pairs={{0,1},{1,0},{2,3},{3,2},{4,5},{5,4},{6,7},{7,6},{8,9},{9,8},{10,11... | collective-permute-start | bytes 786440 | tf_op jit(solution)/shard_map/ppermute | solution.py:419
  26.0 1.6 %collective-permute-start.11 = (f32[2,4,2,8,512]{4,3,2,1,0:T(8,128)S(1)}, f32[2,4,2,8,512]{4,3,2,1,0:T(8,128)S(1)}, u32[]{:S(2)}, u32[]{:S(2)}) collective-permute-start(f32[2,4,2,8,512]{4,3,2,1,0:T(8,128)S(1)} %shard_map.79.refs_2_), channel_id=1, source_target_pairs={{0,1},{1,0},{2,3},{3,2},{4,5},{5,4},{6,7},{7,6},{8,9},{9,8},{10,11... | collective-permute-start | bytes 786440 | tf_op jit(solution)/shard_map/ppermute | solution.py:419

commit v2 on v1

--- a/solution.py
+++ b/solution.py
@@ -188,8 +188,8 @@
     entry = [my_y ^ j for j in range(devices[1])]
 
     def tile(near, far, k, ahead, at, cols):
-        by_x = (near[0], 1) if k < 2 else (far[1], 0)
-        diagonal = (far[k // 2], 1)
+        by_x = (near[0], 1) if k < 2 else (far[0], 1)
+        diagonal = (far[1], k // 2)
         if ahead == 0:
             ref, i = near[k // 2], 0
         elif ahead == 2:
@@ -431,7 +431,7 @@
     first_y, second_x = swapped(first, "gx", 2), swapped(second, "gx", 1)
     first_diagonal, second_diagonal = swapped(first_x, "gx", 2), swapped(second_y, "gx", 1)
     near = [paired(first, first_x), paired(second, second_y)]
-    far = [paired(first_y, first_diagonal), paired(second_x, second_diagonal)]
+    far = [paired(first_y, second_x), paired(first_diagonal, second_diagonal)]
     others = [swapped(pair, "gz", 1) for pair in (*near, *far)]
 
     field = pltpu.VMEM((lanes // 128, 512, 128), F32)

time: 35.5 us -> 34.8 us (0.980)
  waiting for transfers between devices: 12.6 us -> 11.6 us
    ppermute x13, waiting for transfers between devices: 12.6 us -> 11.6 us  [swapped(): return lax.ppermute(block, axis, [(i, i ^ mask) for i in range(count)])]
  transfers between devices with their start and end apart: 13 -> 13, of which waited for: 7 -> 8; matrix products, arithmetic and copies ran while one was open for 0% -> 0% of each run, Pallas kernels for 0% -> 0%
where the time goes in v2:
time: 34.8 us; the launch traced here: 34.5 us
  starting transfers between devices  13.5 us (39%)
  waiting for transfers between devices  11.6 us (33%)
  Pallas kernels  7.84 us (23%)
  other arithmetic  0.83 us (2%)
  between operations  0.74 us (2%)
    ppermute x13, starting transfers between devices, swapped(): return lax.ppermute(block, axis, [(i, i ^ mask) for i in range(count)])  13.5 us
    ppermute x13, waiting for transfers between devices, swapped(): return lax.ppermute(block, axis, [(i, i ^ mask) for i in range(count)])  11.6 us
    pallas_call x1, Pallas kernels, whole_body(): pl.pallas_call(functools.partial(whole_kernel, devices, weights, derivati...  7.72 us
    concatenate x1, other arithmetic, whole_body(): block = jnp.concatenate([velocity, reaction[None]], axis=0)  0.83 us
  transfers between devices with their start and end apart: 13, of which 8 were waited for; matrix products, arithmetic and copies ran while one was open for 0% of the time, Pallas kernels for 0%

profile of v2, /device:TPU:0, one launch (start us, length us, event | category | flops | bytes accessed | tf_op | source)
XLA Modules:
  0.0 34.5 jit_solution(17589713909730029877)
XLA Ops:
  0.6 0.8 %pad_maximum_fusion.refs_0_ = f32[4,2,1,4,512]{4,3,2,1,0:T(4,128)S(1)} fusion(f32[1,2,1,4,512]{4,3,2,1,0:T(4,128)} %bitcast.1, f32[3,2,1,4,512]{4,3,2,1,0:T(4,128)} %param.5), kind=kLoop, calls=%fused_computation | loop fusion | flops 16384 | bytes 131072 | tf_op jit(solution)/shard_map/concatenate | solution.py:421
  1.5 5.1 %collective-permute-start.2 = (f32[4,2,1,4,512]{4,3,2,1,0:T(4,128)S(1)}, f32[4,2,1,4,512]{4,3,2,1,0:T(4,128)S(1)}, u32[]{:S(2)}, u32[]{:S(2)}) collective-permute-start(f32[4,2,1,4,512]{4,3,2,1,0:T(4,128)S(1)} %pad_maximum_fusion.refs_0_), channel_id=1, source_target_pairs={{0,6},{2,4},{4,2},{6,0},{1,7},{3,5},{5,3},{7,1},{8,14},{10,12},{12... | collective-permute-start | bytes 196616 | tf_op jit(solution)/shard_map/ppermute | solution.py:419
  6.6 0.0 collective-permute-start.1
  6.6 0.6 %collective-permute-start = (f32[4,2,1,4,512]{4,3,2,1,0:T(4,128)S(1)}, f32[4,2,1,4,512]{4,3,2,1,0:T(4,128)S(1)}, u32[]{:S(2)}, u32[]{:S(2)}) collective-permute-start(f32[4,2,1,4,512]{4,3,2,1,0:T(4,128)S(1)} %pad_maximum_fusion.refs_0_), channel_id=1, source_target_pairs={{0,2},{2,0},{4,6},{6,4},{1,3},{3,1},{5,7},{7,5},{8,10},{10,8},{12,... | collective-permute-start | bytes 196616 | tf_op jit(solution)/shard_map/ppermute | solution.py:419
  7.2 1.9 %collective-permute-done.2.refs_3_ = f32[4,2,1,4,512]{4,3,2,1,0:T(4,128)S(1)} collective-permute-done((f32[4,2,1,4,512]{4,3,2,1,0:T(4,128)S(1)}, f32[4,2,1,4,512]{4,3,2,1,0:T(4,128)S(1)}, u32[]{:S(2)}, u32[]{:S(2)}) %collective-permute-start.2) | collective-permute-done | bytes 65568 | tf_op jit(solution)/shard_map/ppermute | solution.py:419
  9.2 3.0 %collective-permute-done.1.refs_2_ = f32[4,2,1,4,512]{4,3,2,1,0:T(4,128)S(1)} collective-permute-done((f32[4,2,1,4,512]{4,3,2,1,0:T(4,128)S(1)}, f32[4,2,1,4,512]{4,3,2,1,0:T(4,128)S(1)}, u32[]{:S(2)}, u32[]{:S(2)}) %collective-permute-start.1) | collective-permute-done | bytes 65568 | tf_op jit(solution)/shard_map/ppermute | solution.py:419
  12.2 0.0 collective-permute-done.refs_1_
  12.2 1.6 %collective-permute-start.3 = (f32[4,2,8,512]{3,2,1,0:T(8,128)S(1)}, f32[4,2,8,512]{3,2,1,0:T(8,128)S(1)}, u32[]{:S(2)}, u32[]{:S(2)}) collective-permute-start(f32[4,2,8,512]{3,2,1,0:T(8,128)S(1)} %get-tuple-element.5.first), channel_id=1, source_target_pairs={{0,8},{8,0},{16,24},{24,16},{1,9},{9,1},{17,25},{25,17},{2,10},{10... | collective-permute-start | bytes 393224 | tf_op jit(solution)/shard_map/ppermute | solution.py:419
  13.8 1.5 %collective-permute-start.4 = (f32[4,2,8,512]{3,2,1,0:T(8,128)S(1)}, f32[4,2,8,512]{3,2,1,0:T(8,128)S(1)}, u32[]{:S(2)}, u32[]{:S(2)}) collective-permute-start(f32[4,2,8,512]{3,2,1,0:T(8,128)S(1)} %get-tuple-element.6.first), channel_id=1, source_target_pairs={{0,16},{8,24},{16,0},{24,8},{1,17},{9,25},{17,1},{25,9},{2,18},{10... | collective-permute-start | bytes 393224 | tf_op jit(solution)/shard_map/ppermute | solution.py:419
  15.3 0.5 %collective-permute-start.5 = (f32[4,2,8,512]{3,2,1,0:T(8,128)S(1)}, f32[4,2,8,512]{3,2,1,0:T(8,128)S(1)}, u32[]{:S(2)}, u32[]{:S(2)}) collective-permute-start(f32[4,2,8,512]{3,2,1,0:T(8,128)S(1)} %get-tuple-element.5.first), channel_id=1, source_target_pairs={{0,16},{8,24},{16,0},{24,8},{1,17},{9,25},{17,1},{25,9},{2,18},{10... | collective-permute-start | bytes 393224 | tf_op jit(solution)/shard_map/ppermute | solution.py:419
  15.8 0.5 %collective-permute-start.6 = (f32[4,2,8,512]{3,2,1,0:T(8,128)S(1)}, f32[4,2,8,512]{3,2,1,0:T(8,128)S(1)}, u32[]{:S(2)}, u32[]{:S(2)}) collective-permute-start(f32[4,2,8,512]{3,2,1,0:T(8,128)S(1)} %get-tuple-element.6.first), channel_id=1, source_target_pairs={{0,8},{8,0},{16,24},{24,16},{1,9},{9,1},{17,25},{25,17},{2,10},{10... | collective-permute-start | bytes 393224 | tf_op jit(solution)/shard_map/ppermute | solution.py:419
  16.4 1.3 %collective-permute-done.3.second = f32[4,2,8,512]{3,2,1,0:T(8,128)S(1)} collective-permute-done((f32[4,2,8,512]{3,2,1,0:T(8,128)S(1)}, f32[4,2,8,512]{3,2,1,0:T(8,128)S(1)}, u32[]{:S(2)}, u32[]{:S(2)}) %collective-permute-start.3) | collective-permute-done | bytes 131104 | tf_op jit(solution)/shard_map/ppermute | solution.py:419
  17.7 1.5 %collective-permute-start.7 = (f32[4,2,8,512]{3,2,1,0:T(8,128)S(1)}, f32[4,2,8,512]{3,2,1,0:T(8,128)S(1)}, u32[]{:S(2)}, u32[]{:S(2)}) collective-permute-start(f32[4,2,8,512]{3,2,1,0:T(8,128)S(1)} %collective-permute-done.3.second), channel_id=1, source_target_pairs={{0,16},{8,24},{16,0},{24,8},{1,17},{9,25},{17,1},{25,9},{2,18},{10... | collective-permute-start | bytes 393224 | tf_op jit(solution)/shard_map/ppermute | solution.py:419
  19.2 1.0 %collective-permute-done.4.second = f32[4,2,8,512]{3,2,1,0:T(8,128)S(1)} collective-permute-done((f32[4,2,8,512]{3,2,1,0:T(8,128)S(1)}, f32[4,2,8,512]{3,2,1,0:T(8,128)S(1)}, u32[]{:S(2)}, u32[]{:S(2)}) %collective-permute-start.4) | collective-permute-done | bytes 131104 | tf_op jit(solution)/shard_map/ppermute | solution.py:419
  20.2 1.4 %collective-permute-start.8 = (f32[4,2,8,512]{3,2,1,0:T(8,128)S(1)}, f32[4,2,8,512]{3,2,1,0:T(8,128)S(1)}, u32[]{:S(2)}, u32[]{:S(2)}) collective-permute-start(f32[4,2,8,512]{3,2,1,0:T(8,128)S(1)} %collective-permute-done.4.second), channel_id=1, source_target_pairs={{0,8},{8,0},{16,24},{24,16},{1,9},{9,1},{17,25},{25,17},{2,10},{10... | collective-permute-start | bytes 393224 | tf_op jit(solution)/shard_map/ppermute | solution.py:419
  21.7 0.1 collective-permute-start.10
  21.8 1.2 %collective-permute-done.5.first = f32[4,2,8,512]{3,2,1,0:T(8,128)S(1)} collective-permute-done((f32[4,2,8,512]{3,2,1,0:T(8,128)S(1)}, f32[4,2,8,512]{3,2,1,0:T(8,128)S(1)}, u32[]{:S(2)}, u32[]{:S(2)}) %collective-permute-start.5) | collective-permute-done | bytes 131104 | tf_op jit(solution)/shard_map/ppermute | solution.py:419
  23.0 0.0 collective-permute-done.6.second
  23.0 0.1 collective-permute-start.11
  23.1 0.0 copy-start
  23.1 0.0 copy-start.1
  23.1 0.0 copy-start.2
  23.1 0.6 %collective-permute-start.9 = (f32[2,4,2,8,512]{4,3,2,1,0:T(8,128)S(1)}, f32[2,4,2,8,512]{4,3,2,1,0:T(8,128)S(1)}, u32[]{:S(2)}, u32[]{:S(2)}) collective-permute-start(f32[2,4,2,8,512]{4,3,2,1,0:T(8,128)S(1)} %shard_map.77.refs_0_), channel_id=1, source_target_pairs={{0,1},{1,0},{2,3},{3,2},{4,5},{5,4},{6,7},{7,6},{8,9},{9,8},{10,11... | collective-permute-start | bytes 786440 | tf_op jit(solution)/shard_map/ppermute | solution.py:419
  23.7 0.7 %collective-permute-done.7.first = f32[4,2,8,512]{3,2,1,0:T(8,128)S(1)} collective-permute-done((f32[4,2,8,512]{3,2,1,0:T(8,128)S(1)}, f32[4,2,8,512]{3,2,1,0:T(8,128)S(1)}, u32[]{:S(2)}, u32[]{:S(2)}) %collective-permute-start.7) | collective-permute-done | bytes 131104 | tf_op jit(solution)/shard_map/ppermute | solution.py:419
  24.4 0.8 %collective-permute-done.8.second = f32[4,2,8,512]{3,2,1,0:T(8,128)S(1)} collective-permute-done((f32[4,2,8,512]{3,2,1,0:T(8,128)S(1)}, f32[4,2,8,512]{3,2,1,0:T(8,128)S(1)}, u32[]{:S(2)}, u32[]{:S(2)}) %collective-permute-start.8) | collective-permute-done | bytes 131104 | tf_op jit(solution)/shard_map/ppermute | solution.py:419
  25.2 0.1 collective-permute-start.12
  25.3 0.0 collective-permute-done.10.refs_5_
  25.3 0.0 collective-permute-done.11.refs_6_
  25.3 0.0 collective-permute-done.9.refs_4_
  25.3 1.5 %collective-permute-done.12.refs_7_ = f32[2,4,2,8,512]{4,3,2,1,0:T(8,128)S(1)} collective-permute-done((f32[2,4,2,8,512]{4,3,2,1,0:T(8,128)S(1)}, f32[2,4,2,8,512]{4,3,2,1,0:T(8,128)S(1)}, u32[]{:S(2)}, u32[]{:S(2)}) %collective-permute-start.12) | collective-permute-done | bytes 262176 | tf_op jit(solution)/shard_map/ppermute | solution.py:419
  26.8 0.0 copy-done
  26.8 0.0 copy-done.1
  26.8 0.0 copy-done.2
  26.8 7.7 %shard_map.81 = (f32[3,2,1,4,512]{4,3,2,1,0:T(4,128)}, f32[2,1,4,512]{3,2,1,0:T(4,128)}, f32[2,1,4,512]{3,2,1,0:T(4,128)}) custom-call(f32[2,4,2,8,512]{4,3,2,1,0:T(8,128)S(1)} %shard_map.77.refs_0_, f32[2,4,2,8,512]{4,3,2,1,0:T(8,128)S(1)} %shard_map.78.refs_1_, f32[2,4,2,8,512]{4,3,2,1,0:T(8,128)S(1)} %shard_map.79.refs_2_, ...), custom_call_target="tpu_custom_call" | custom-call | tf_op jit(solution)/shard_map/pallas_call | solution.py:441
  (5 shorter events, 0.1 us)
Async XLA Ops:
  1.5 7.7 %collective-permute-start.2 = (f32[4,2,1,4,512]{4,3,2,1,0:T(4,128)S(1)}, f32[4,2,1,4,512]{4,3,2,1,0:T(4,128)S(1)}, u32[]{:S(2)}, u32[]{:S(2)}) collective-permute-start(f32[4,2,1,4,512]{4,3,2,1,0:T(4,128)S(1)} %pad_maximum_fusion.refs_0_), channel_id=1, source_target_pairs={{0,6},{2,4},{4,2},{6,0},{1,7},{3,5},{5,3},{7,1},{8,14},{10,12},{12... | collective-permute-start | bytes 196616 | tf_op jit(solution)/shard_map/ppermute | solution.py:419
  6.6 5.6 %collective-permute-start.1 = (f32[4,2,1,4,512]{4,3,2,1,0:T(4,128)S(1)}, f32[4,2,1,4,512]{4,3,2,1,0:T(4,128)S(1)}, u32[]{:S(2)}, u32[]{:S(2)}) collective-permute-start(f32[4,2,1,4,512]{4,3,2,1,0:T(4,128)S(1)} %pad_maximum_fusion.refs_0_), channel_id=1, source_target_pairs={{0,4},{2,6},{4,0},{6,2},{1,5},{3,7},{5,1},{7,3},{8,12},{10,14},{12... | collective-permute-start | bytes 196616 | tf_op jit(solution)/shard_map/ppermute | solution.py:419
  6.6 5.6 %collective-permute-start = (f32[4,2,1,4,512]{4,3,2,1,0:T(4,128)S(1)}, f32[4,2,1,4,512]{4,3,2,1,0:T(4,128)S(1)}, u32[]{:S(2)}, u32[]{:S(2)}) collective-permute-start(f32[4,2,1,4,512]{4,3,2,1,0:T(4,128)S(1)} %pad_maximum_fusion.refs_0_), channel_id=1, source_target_pairs={{0,2},{2,0},{4,6},{6,4},{1,3},{3,1},{5,7},{7,5},{8,10},{10,8},{12,... | collective-permute-start | bytes 196616 | tf_op jit(solution)/shard_map/ppermute | solution.py:419
  12.2 5.5 %collective-permute-start.3 = (f32[4,2,8,512]{3,2,1,0:T(8,128)S(1)}, f32[4,2,8,512]{3,2,1,0:T(8,128)S(1)}, u32[]{:S(2)}, u32[]{:S(2)}) collective-permute-start(f32[4,2,8,512]{3,2,1,0:T(8,128)S(1)} %get-tuple-element.5.first), channel_id=1, source_target_pairs={{0,8},{8,0},{16,24},{24,16},{1,9},{9,1},{17,25},{25,17},{2,10},{10... | collective-permute-start | bytes 393224 | tf_op jit(solution)/shard_map/ppermute | solution.py:419
  13.8 6.4 %collective-permute-start.4 = (f32[4,2,8,512]{3,2,1,0:T(8,128)S(1)}, f32[4,2,8,512]{3,2,1,0:T(8,128)S(1)}, u32[]{:S(2)}, u32[]{:S(2)}) collective-permute-start(f32[4,2,8,512]{3,2,1,0:T(8,128)S(1)} %get-tuple-element.6.first), channel_id=1, source_target_pairs={{0,16},{8,24},{16,0},{24,8},{1,17},{9,25},{17,1},{25,9},{2,18},{10... | collective-permute-start | bytes 393224 | tf_op jit(solution)/shard_map/ppermute | solution.py:419
  15.3 7.7 %collective-permute-start.5 = (f32[4,2,8,512]{3,2,1,0:T(8,128)S(1)}, f32[4,2,8,512]{3,2,1,0:T(8,128)S(1)}, u32[]{:S(2)}, u32[]{:S(2)}) collective-permute-start(f32[4,2,8,512]{3,2,1,0:T(8,128)S(1)} %get-tuple-element.5.first), channel_id=1, source_target_pairs={{0,16},{8,24},{16,0},{24,8},{1,17},{9,25},{17,1},{25,9},{2,18},{10... | collective-permute-start | bytes 393224 | tf_op jit(solution)/shard_map/ppermute | solution.py:419
  15.8 7.2 %collective-permute-start.6 = (f32[4,2,8,512]{3,2,1,0:T(8,128)S(1)}, f32[4,2,8,512]{3,2,1,0:T(8,128)S(1)}, u32[]{:S(2)}, u32[]{:S(2)}) collective-permute-start(f32[4,2,8,512]{3,2,1,0:T(8,128)S(1)} %get-tuple-element.6.first), channel_id=1, source_target_pairs={{0,8},{8,0},{16,24},{24,16},{1,9},{9,1},{17,25},{25,17},{2,10},{10... | collective-permute-start | bytes 393224 | tf_op jit(solution)/shard_map/ppermute | solution.py:419
  17.7 6.7 %collective-permute-start.7 = (f32[4,2,8,512]{3,2,1,0:T(8,128)S(1)}, f32[4,2,8,512]{3,2,1,0:T(8,128)S(1)}, u32[]{:S(2)}, u32[]{:S(2)}) collective-permute-start(f32[4,2,8,512]{3,2,1,0:T(8,128)S(1)} %collective-permute-done.3.second), channel_id=1, source_target_pairs={{0,16},{8,24},{16,0},{24,8},{1,17},{9,25},{17,1},{25,9},{2,18},{10... | collective-permute-start | bytes 393224 | tf_op jit(solution)/shard_map/ppermute | solution.py:419
  20.2 5.0 %collective-permute-start.8 = (f32[4,2,8,512]{3,2,1,0:T(8,128)S(1)}, f32[4,2,8,512]{3,2,1,0:T(8,128)S(1)}, u32[]{:S(2)}, u32[]{:S(2)}) collective-permute-start(f32[4,2,8,512]{3,2,1,0:T(8,128)S(1)} %collective-permute-done.4.second), channel_id=1, source_target_pairs={{0,8},{8,0},{16,24},{24,16},{1,9},{9,1},{17,25},{25,17},{2,10},{10... | collective-permute-start | bytes 393224 | tf_op jit(solution)/shard_map/ppermute | solution.py:419
  21.7 3.6 %collective-permute-start.10 = (f32[2,4,2,8,512]{4,3,2,1,0:T(8,128)S(1)}, f32[2,4,2,8,512]{4,3,2,1,0:T(8,128)S(1)}, u32[]{:S(2)}, u32[]{:S(2)}) collective-permute-start(f32[2,4,2,8,512]{4,3,2,1,0:T(8,128)S(1)} %shard_map.78.refs_1_), channel_id=1, source_target_pairs={{0,1},{1,0},{2,3},{3,2},{4,5},{5,4},{6,7},{7,6},{8,9},{9,8},{10,11... | collective-permute-start | bytes 786440 | tf_op jit(solution)/shard_map/ppermute | solution.py:419
  23.0 2.3 %collective-permute-start.11 = (f32[2,4,2,8,512]{4,3,2,1,0:T(8,128)S(1)}, f32[2,4,2,8,512]{4,3,2,1,0:T(8,128)S(1)}, u32[]{:S(2)}, u32[]{:S(2)}) collective-permute-start(f32[2,4,2,8,512]{4,3,2,1,0:T(8,128)S(1)} %shard_map.79.refs_2_), channel_id=1, source_target_pairs={{0,1},{1,0},{2,3},{3,2},{4,5},{5,4},{6,7},{7,6},{8,9},{9,8},{10,11... | collective-permute-start | bytes 786440 | tf_op jit(solution)/shard_map/ppermute | solution.py:419
  23.1 3.7 %copy-start = (bf16[256,384]{1,0:T(8,128)(2,1)S(1)}, bf16[256,384]{1,0:T(8,128)(2,1)}, u32[]{:S(2)}) copy-start(bf16[256,384]{1,0:T(8,128)(2,1)} %constant.8.clone.refs_10_) | copy-start | bytes 589828
  23.1 3.7 %copy-start.1 = (bf16[384,192]{1,0:T(8,128)(2,1)S(1)}, bf16[384,192]{1,0:T(8,128)(2,1)}, u32[]{:S(2)}) copy-start(bf16[384,192]{1,0:T(8,128)(2,1)} %constant.7.clone.refs_9_) | copy-start | bytes 442372
  23.1 3.7 %copy-start.2 = (f32[128,128]{1,0:T(8,128)S(1)}, f32[128,128]{1,0:T(8,128)}, u32[]{:S(2)}) copy-start(f32[128,128]{1,0:T(8,128)} %constant.6.clone.refs_8_) | copy-start | bytes 196612
  23.1 2.2 %collective-permute-start.9 = (f32[2,4,2,8,512]{4,3,2,1,0:T(8,128)S(1)}, f32[2,4,2,8,512]{4,3,2,1,0:T(8,128)S(1)}, u32[]{:S(2)}, u32[]{:S(2)}) collective-permute-start(f32[2,4,2,8,512]{4,3,2,1,0:T(8,128)S(1)} %shard_map.77.refs_0_), channel_id=1, source_target_pairs={{0,1},{1,0},{2,3},{3,2},{4,5},{5,4},{6,7},{7,6},{8,9},{9,8},{10,11... | collective-permute-start | bytes 786440 | tf_op jit(solution)/shard_map/ppermute | solution.py:419
  25.2 1.6 %collective-permute-start.12 = (f32[2,4,2,8,512]{4,3,2,1,0:T(8,128)S(1)}, f32[2,4,2,8,512]{4,3,2,1,0:T(8,128)S(1)}, u32[]{:S(2)}, u32[]{:S(2)}) collective-permute-start(f32[2,4,2,8,512]{4,3,2,1,0:T(8,128)S(1)} %shard_map.80.refs_3_), channel_id=1, source_target_pairs={{0,1},{1,0},{2,3},{3,2},{4,5},{5,4},{6,7},{7,6},{8,9},{9,8},{10,11... | collective-permute-start | bytes 786440 | tf_op jit(solution)/shard_map/ppermute | solution.py:419

commit v3 on v2

--- a/solution.py
+++ b/solution.py
@@ -171,7 +171,7 @@
         near, far, near_other, far_other, cross_ref, matrix_ref, pair_ref,
         vel_out, pre_out, res_out,
         u, v, xs, rm, w, dinv, z, r, y, s, p, x, flip, vel_own, pre_own, res_own, sems,
-    ) = [refs[0:2], refs[2:4], refs[4:6], refs[6:8], *refs[8:]]
+    ) = [refs[0:2], refs[2:5], refs[5:7], refs[7:10], *refs[10:]]
     my_y, my_z = lax.axis_index("gy"), lax.axis_index("gz")
     fields = u.shape[0]
     halves = range(u.shape[1])
@@ -188,17 +188,16 @@
     entry = [my_y ^ j for j in range(devices[1])]
 
     def tile(near, far, k, ahead, at, cols):
-        by_x = (near[0], 1) if k < 2 else (far[0], 1)
-        diagonal = (far[1], k // 2)
         if ahead == 0:
-            ref, i = near[k // 2], 0
-        elif ahead == 2:
+            return near[k // 2][0, at, k % 2, :, cols]
+        if ahead == 2:
             ref, i = (far[0], 0) if k < 2 else (near[1], 1)
-        else:
-            first, second = (by_x, diagonal) if ahead == 1 else (diagonal, by_x)
-            first, second = (ref[i, at, k % 2, :, cols] for ref, i in (first, second))
-            return jnp.where(is_even, first, second)
-        return ref[i, at, k % 2, :, cols]
+            return ref[i, at, k % 2, :, cols]
+        ref = near[0] if k < 2 else far[0]
+        by_x, diagonal = ref[1, at, k % 2, :, cols], far[1 + k // 2][at, k % 2, :, cols]
+        if ahead == 1:
+            return jnp.where(is_even, by_x, diagonal)
+        return jnp.where(is_even, diagonal, by_x)
 
     def to_lanes(k, chunk):
         cols = pl.ds(128 * chunk, 128)
@@ -431,7 +430,7 @@
     first_y, second_x = swapped(first, "gx", 2), swapped(second, "gx", 1)
     first_diagonal, second_diagonal = swapped(first_x, "gx", 2), swapped(second_y, "gx", 1)
     near = [paired(first, first_x), paired(second, second_y)]
-    far = [paired(first_y, second_x), paired(first_diagonal, second_diagonal)]
+    far = [paired(first_y, second_x), first_diagonal, second_diagonal]
     others = [swapped(pair, "gz", 1) for pair in (*near, *far)]
 
     field = pltpu.VMEM((lanes // 128, 512, 128), F32)
@@ -445,7 +444,7 @@
             jax.ShapeDtypeStruct(reaction.shape, F32),
             jax.ShapeDtypeStruct(reaction.shape, F32),
         ),
-        in_specs=[vmem] * 11,
+        in_specs=[vmem] * 13,
         out_specs=(hbm, hbm, hbm),
         scratch_shapes=[three, three, pltpu.VMEM((fields, 2, 512, lanes), BF16)]
         + [field] * 7

time: 34.8 us -> 35.4 us (1.017)
  starting transfers between devices: 13.5 us -> 15.1 us
  waiting for transfers between devices: 11.6 us -> 10.7 us
    ppermute x13 -> x14, starting transfers between devices: 13.5 us -> 15.1 us  [swapped(): return lax.ppermute(block, axis, [(i, i ^ mask) for i in range(count)])]
    ppermute x13 -> x14, waiting for transfers between devices: 11.6 us -> 10.7 us  [swapped(): return lax.ppermute(block, axis, [(i, i ^ mask) for i in range(count)])]
  transfers between devices with their start and end apart: 13 -> 14, of which waited for: 8 -> 6; matrix products, arithmetic and copies ran while one was open for 0% -> 0% of each run, Pallas kernels for 0% -> 0%
where the time goes in v3:
time: 35.4 us; the launch traced here: 35.2 us
  starting transfers between devices  15.1 us (43%)
  waiting for transfers between devices  10.7 us (30%)
  Pallas kernels  7.8 us (22%)
  other arithmetic  0.83 us (2%)
  between operations  0.73 us (2%)
    ppermute x14, starting transfers between devices, swapped(): return lax.ppermute(block, axis, [(i, i ^ mask) for i in range(count)])  15.1 us
    ppermute x14, waiting for transfers between devices, swapped(): return lax.ppermute(block, axis, [(i, i ^ mask) for i in range(count)])  10.7 us
    pallas_call x1, Pallas kernels, whole_body(): pl.pallas_call(functools.partial(whole_kernel, devices, weights, derivati...  7.69 us
    concatenate x1, other arithmetic, whole_body(): block = jnp.concatenate([velocity, reaction[None]], axis=0)  0.83 us
  transfers between devices with their start and end apart: 14, of which 6 were waited for; matrix products, arithmetic and copies ran while one was open for 0% of the time, Pallas kernels for 0%

profile of v3, /device:TPU:0, one launch (start us, length us, event | category | flops | bytes accessed | tf_op | source)
XLA Modules:
  0.0 35.2 jit_solution(4794917049684924325)
XLA Ops:
  0.6 0.8 %pad_maximum_fusion.refs_0_ = f32[4,2,1,4,512]{4,3,2,1,0:T(4,128)S(1)} fusion(f32[1,2,1,4,512]{4,3,2,1,0:T(4,128)} %bitcast.1, f32[3,2,1,4,512]{4,3,2,1,0:T(4,128)} %param.5), kind=kLoop, calls=%fused_computation | loop fusion | flops 16384 | bytes 131072 | tf_op jit(solution)/shard_map/concatenate | solution.py:420
  1.5 5.1 %collective-permute-start.2 = (f32[4,2,1,4,512]{4,3,2,1,0:T(4,128)S(1)}, f32[4,2,1,4,512]{4,3,2,1,0:T(4,128)S(1)}, u32[]{:S(2)}, u32[]{:S(2)}) collective-permute-start(f32[4,2,1,4,512]{4,3,2,1,0:T(4,128)S(1)} %pad_maximum_fusion.refs_0_), channel_id=1, source_target_pairs={{0,6},{2,4},{4,2},{6,0},{1,7},{3,5},{5,3},{7,1},{8,14},{10,12},{12... | collective-permute-start | bytes 196616 | tf_op jit(solution)/shard_map/ppermute | solution.py:418
  6.6 0.0 collective-permute-start.1
  6.6 0.6 %collective-permute-start = (f32[4,2,1,4,512]{4,3,2,1,0:T(4,128)S(1)}, f32[4,2,1,4,512]{4,3,2,1,0:T(4,128)S(1)}, u32[]{:S(2)}, u32[]{:S(2)}) collective-permute-start(f32[4,2,1,4,512]{4,3,2,1,0:T(4,128)S(1)} %pad_maximum_fusion.refs_0_), channel_id=1, source_target_pairs={{0,2},{2,0},{4,6},{6,4},{1,3},{3,1},{5,7},{7,5},{8,10},{10,8},{12,... | collective-permute-start | bytes 196616 | tf_op jit(solution)/shard_map/ppermute | solution.py:418
  7.2 1.9 %collective-permute-done.2.refs_3_ = f32[4,2,1,4,512]{4,3,2,1,0:T(4,128)S(1)} collective-permute-done((f32[4,2,1,4,512]{4,3,2,1,0:T(4,128)S(1)}, f32[4,2,1,4,512]{4,3,2,1,0:T(4,128)S(1)}, u32[]{:S(2)}, u32[]{:S(2)}) %collective-permute-start.2) | collective-permute-done | bytes 65568 | tf_op jit(solution)/shard_map/ppermute | solution.py:418
  9.2 3.0 %collective-permute-done.1.refs_2_ = f32[4,2,1,4,512]{4,3,2,1,0:T(4,128)S(1)} collective-permute-done((f32[4,2,1,4,512]{4,3,2,1,0:T(4,128)S(1)}, f32[4,2,1,4,512]{4,3,2,1,0:T(4,128)S(1)}, u32[]{:S(2)}, u32[]{:S(2)}) %collective-permute-start.1) | collective-permute-done | bytes 65568 | tf_op jit(solution)/shard_map/ppermute | solution.py:418
  12.2 0.0 collective-permute-done.refs_1_
  12.2 1.6 %collective-permute-start.4 = (f32[4,2,8,512]{3,2,1,0:T(8,128)S(1)}, f32[4,2,8,512]{3,2,1,0:T(8,128)S(1)}, u32[]{:S(2)}, u32[]{:S(2)}) collective-permute-start(f32[4,2,8,512]{3,2,1,0:T(8,128)S(1)} %get-tuple-element.6.first), channel_id=1, source_target_pairs={{0,16},{8,24},{16,0},{24,8},{1,17},{9,25},{17,1},{25,9},{2,18},{10... | collective-permute-start | bytes 393224 | tf_op jit(solution)/shard_map/ppermute | solution.py:418
  13.8 1.5 %collective-permute-start.3 = (f32[4,2,8,512]{3,2,1,0:T(8,128)S(1)}, f32[4,2,8,512]{3,2,1,0:T(8,128)S(1)}, u32[]{:S(2)}, u32[]{:S(2)}) collective-permute-start(f32[4,2,8,512]{3,2,1,0:T(8,128)S(1)} %get-tuple-element.5.first), channel_id=1, source_target_pairs={{0,8},{8,0},{16,24},{24,16},{1,9},{9,1},{17,25},{25,17},{2,10},{10... | collective-permute-start | bytes 393224 | tf_op jit(solution)/shard_map/ppermute | solution.py:418
  15.3 0.5 %collective-permute-start.5 = (f32[4,2,8,512]{3,2,1,0:T(8,128)S(1)}, f32[4,2,8,512]{3,2,1,0:T(8,128)S(1)}, u32[]{:S(2)}, u32[]{:S(2)}) collective-permute-start(f32[4,2,8,512]{3,2,1,0:T(8,128)S(1)} %get-tuple-element.5.first), channel_id=1, source_target_pairs={{0,16},{8,24},{16,0},{24,8},{1,17},{9,25},{17,1},{25,9},{2,18},{10... | collective-permute-start | bytes 393224 | tf_op jit(solution)/shard_map/ppermute | solution.py:418
  15.8 0.5 %collective-permute-start.6 = (f32[4,2,8,512]{3,2,1,0:T(8,128)S(1)}, f32[4,2,8,512]{3,2,1,0:T(8,128)S(1)}, u32[]{:S(2)}, u32[]{:S(2)}) collective-permute-start(f32[4,2,8,512]{3,2,1,0:T(8,128)S(1)} %get-tuple-element.6.first), channel_id=1, source_target_pairs={{0,8},{8,0},{16,24},{24,16},{1,9},{9,1},{17,25},{25,17},{2,10},{10... | collective-permute-start | bytes 393224 | tf_op jit(solution)/shard_map/ppermute | solution.py:418
  16.4 1.4 %collective-permute-done.4.second = f32[4,2,8,512]{3,2,1,0:T(8,128)S(1)} collective-permute-done((f32[4,2,8,512]{3,2,1,0:T(8,128)S(1)}, f32[4,2,8,512]{3,2,1,0:T(8,128)S(1)}, u32[]{:S(2)}, u32[]{:S(2)}) %collective-permute-start.4) | collective-permute-done | bytes 131104 | tf_op jit(solution)/shard_map/ppermute | solution.py:418
  17.7 0.1 collective-permute-start.10
  17.8 2.5 %collective-permute-start.8 = (f32[4,2,8,512]{3,2,1,0:T(8,128)S(1)}, f32[4,2,8,512]{3,2,1,0:T(8,128)S(1)}, u32[]{:S(2)}, u32[]{:S(2)}) collective-permute-start(f32[4,2,8,512]{3,2,1,0:T(8,128)S(1)} %collective-permute-done.4.second), channel_id=1, source_target_pairs={{0,8},{8,0},{16,24},{24,16},{1,9},{9,1},{17,25},{25,17},{2,10},{10... | collective-permute-start | bytes 393224 | tf_op jit(solution)/shard_map/ppermute | solution.py:418
  20.3 0.0 collective-permute-done.3.second
  20.3 1.5 %collective-permute-start.7 = (f32[4,2,8,512]{3,2,1,0:T(8,128)S(1)}, f32[4,2,8,512]{3,2,1,0:T(8,128)S(1)}, u32[]{:S(2)}, u32[]{:S(2)}) collective-permute-start(f32[4,2,8,512]{3,2,1,0:T(8,128)S(1)} %collective-permute-done.3.second), channel_id=1, source_target_pairs={{0,16},{8,24},{16,0},{24,8},{1,17},{9,25},{17,1},{25,9},{2,18},{10... | collective-permute-start | bytes 393224 | tf_op jit(solution)/shard_map/ppermute | solution.py:418
  21.9 0.0 collective-permute-done.5.first
  21.9 0.0 collective-permute-done.6.second
  21.9 0.0 copy-start
  21.9 0.0 copy-start.1
  21.9 0.0 copy-start.2
  21.9 0.1 collective-permute-start.11
  22.0 0.6 %collective-permute-start.9 = (f32[2,4,2,8,512]{4,3,2,1,0:T(8,128)S(1)}, f32[2,4,2,8,512]{4,3,2,1,0:T(8,128)S(1)}, u32[]{:S(2)}, u32[]{:S(2)}) collective-permute-start(f32[2,4,2,8,512]{4,3,2,1,0:T(8,128)S(1)} %shard_map.77.refs_0_), channel_id=1, source_target_pairs={{0,1},{1,0},{2,3},{3,2},{4,5},{5,4},{6,7},{7,6},{8,9},{9,8},{10,11... | collective-permute-start | bytes 786440 | tf_op jit(solution)/shard_map/ppermute | solution.py:418
  22.6 3.3 %collective-permute-done.7.refs_3_ = f32[4,2,8,512]{3,2,1,0:T(8,128)S(1)} collective-permute-done((f32[4,2,8,512]{3,2,1,0:T(8,128)S(1)}, f32[4,2,8,512]{3,2,1,0:T(8,128)S(1)}, u32[]{:S(2)}, u32[]{:S(2)}) %collective-permute-start.7) | collective-permute-done | bytes 131104 | tf_op jit(solution)/shard_map/ppermute | solution.py:418
  25.9 0.0 collective-permute-start.12
  25.9 0.0 collective-permute-done.8.refs_4_
  25.9 0.5 %collective-permute-start.13 = (f32[4,2,8,512]{3,2,1,0:T(8,128)S(1)}, f32[4,2,8,512]{3,2,1,0:T(8,128)S(1)}, u32[]{:S(2)}, u32[]{:S(2)}) collective-permute-start(f32[4,2,8,512]{3,2,1,0:T(8,128)S(1)} %collective-permute-done.8.refs_4_), channel_id=1, source_target_pairs={{0,1},{1,0},{2,3},{3,2},{4,5},{5,4},{6,7},{7,6},{8,9},{9,8},{10,11... | collective-permute-start | bytes 393224 | tf_op jit(solution)/shard_map/ppermute | solution.py:418
  26.4 0.8 %collective-permute-done.12.refs_8_ = f32[4,2,8,512]{3,2,1,0:T(8,128)S(1)} collective-permute-done((f32[4,2,8,512]{3,2,1,0:T(8,128)S(1)}, f32[4,2,8,512]{3,2,1,0:T(8,128)S(1)}, u32[]{:S(2)}, u32[]{:S(2)}) %collective-permute-start.12) | collective-permute-done | bytes 131104 | tf_op jit(solution)/shard_map/ppermute | solution.py:418
  27.3 0.2 collective-permute-done.13.refs_9_
  27.5 0.0 collective-permute-done.10.refs_6_
  27.5 0.0 collective-permute-done.11.refs_7_
  27.5 0.0 collective-permute-done.9.refs_5_
  27.5 0.0 copy-done
  27.5 0.0 copy-done.1
  27.5 0.0 copy-done.2
  27.5 7.7 %shard_map.80 = (f32[3,2,1,4,512]{4,3,2,1,0:T(4,128)}, f32[2,1,4,512]{3,2,1,0:T(4,128)}, f32[2,1,4,512]{3,2,1,0:T(4,128)}) custom-call(f32[2,4,2,8,512]{4,3,2,1,0:T(8,128)S(1)} %shard_map.77.refs_0_, f32[2,4,2,8,512]{4,3,2,1,0:T(8,128)S(1)} %shard_map.78.refs_1_, f32[2,4,2,8,512]{4,3,2,1,0:T(8,128)S(1)} %shard_map.79.refs_2_, ...), custom_call_target="tpu_custom_call" | custom-call | tf_op jit(solution)/shard_map/pallas_call | solution.py:440
  (4 shorter events, 0.1 us)
Async XLA Ops:
  1.5 7.7 %collective-permute-start.2 = (f32[4,2,1,4,512]{4,3,2,1,0:T(4,128)S(1)}, f32[4,2,1,4,512]{4,3,2,1,0:T(4,128)S(1)}, u32[]{:S(2)}, u32[]{:S(2)}) collective-permute-start(f32[4,2,1,4,512]{4,3,2,1,0:T(4,128)S(1)} %pad_maximum_fusion.refs_0_), channel_id=1, source_target_pairs={{0,6},{2,4},{4,2},{6,0},{1,7},{3,5},{5,3},{7,1},{8,14},{10,12},{12... | collective-permute-start | bytes 196616 | tf_op jit(solution)/shard_map/ppermute | solution.py:418
  6.6 5.6 %collective-permute-start.1 = (f32[4,2,1,4,512]{4,3,2,1,0:T(4,128)S(1)}, f32[4,2,1,4,512]{4,3,2,1,0:T(4,128)S(1)}, u32[]{:S(2)}, u32[]{:S(2)}) collective-permute-start(f32[4,2,1,4,512]{4,3,2,1,0:T(4,128)S(1)} %pad_maximum_fusion.refs_0_), channel_id=1, source_target_pairs={{0,4},{2,6},{4,0},{6,2},{1,5},{3,7},{5,1},{7,3},{8,12},{10,14},{12... | collective-permute-start | bytes 196616 | tf_op jit(solution)/shard_map/ppermute | solution.py:418
  6.6 5.6 %collective-permute-start = (f32[4,2,1,4,512]{4,3,2,1,0:T(4,128)S(1)}, f32[4,2,1,4,512]{4,3,2,1,0:T(4,128)S(1)}, u32[]{:S(2)}, u32[]{:S(2)}) collective-permute-start(f32[4,2,1,4,512]{4,3,2,1,0:T(4,128)S(1)} %pad_maximum_fusion.refs_0_), channel_id=1, source_target_pairs={{0,2},{2,0},{4,6},{6,4},{1,3},{3,1},{5,7},{7,5},{8,10},{10,8},{12,... | collective-permute-start | bytes 196616 | tf_op jit(solution)/shard_map/ppermute | solution.py:418
  12.2 5.5 %collective-permute-start.4 = (f32[4,2,8,512]{3,2,1,0:T(8,128)S(1)}, f32[4,2,8,512]{3,2,1,0:T(8,128)S(1)}, u32[]{:S(2)}, u32[]{:S(2)}) collective-permute-start(f32[4,2,8,512]{3,2,1,0:T(8,128)S(1)} %get-tuple-element.6.first), channel_id=1, source_target_pairs={{0,16},{8,24},{16,0},{24,8},{1,17},{9,25},{17,1},{25,9},{2,18},{10... | collective-permute-start | bytes 393224 | tf_op jit(solution)/shard_map/ppermute | solution.py:418
  13.8 6.5 %collective-permute-start.3 = (f32[4,2,8,512]{3,2,1,0:T(8,128)S(1)}, f32[4,2,8,512]{3,2,1,0:T(8,128)S(1)}, u32[]{:S(2)}, u32[]{:S(2)}) collective-permute-start(f32[4,2,8,512]{3,2,1,0:T(8,128)S(1)} %get-tuple-element.5.first), channel_id=1, source_target_pairs={{0,8},{8,0},{16,24},{24,16},{1,9},{9,1},{17,25},{25,17},{2,10},{10... | collective-permute-start | bytes 393224 | tf_op jit(solution)/shard_map/ppermute | solution.py:418
  15.3 6.6 %collective-permute-start.5 = (f32[4,2,8,512]{3,2,1,0:T(8,128)S(1)}, f32[4,2,8,512]{3,2,1,0:T(8,128)S(1)}, u32[]{:S(2)}, u32[]{:S(2)}) collective-permute-start(f32[4,2,8,512]{3,2,1,0:T(8,128)S(1)} %get-tuple-element.5.first), channel_id=1, source_target_pairs={{0,16},{8,24},{16,0},{24,8},{1,17},{9,25},{17,1},{25,9},{2,18},{10... | collective-permute-start | bytes 393224 | tf_op jit(solution)/shard_map/ppermute | solution.py:418
  15.8 6.1 %collective-permute-start.6 = (f32[4,2,8,512]{3,2,1,0:T(8,128)S(1)}, f32[4,2,8,512]{3,2,1,0:T(8,128)S(1)}, u32[]{:S(2)}, u32[]{:S(2)}) collective-permute-start(f32[4,2,8,512]{3,2,1,0:T(8,128)S(1)} %get-tuple-element.6.first), channel_id=1, source_target_pairs={{0,8},{8,0},{16,24},{24,16},{1,9},{9,1},{17,25},{25,17},{2,10},{10... | collective-permute-start | bytes 393224 | tf_op jit(solution)/shard_map/ppermute | solution.py:418
  17.7 9.7 %collective-permute-start.10 = (f32[2,4,2,8,512]{4,3,2,1,0:T(8,128)S(1)}, f32[2,4,2,8,512]{4,3,2,1,0:T(8,128)S(1)}, u32[]{:S(2)}, u32[]{:S(2)}) collective-permute-start(f32[2,4,2,8,512]{4,3,2,1,0:T(8,128)S(1)} %shard_map.78.refs_1_), channel_id=1, source_target_pairs={{0,1},{1,0},{2,3},{3,2},{4,5},{5,4},{6,7},{7,6},{8,9},{9,8},{10,11... | collective-permute-start | bytes 786440 | tf_op jit(solution)/shard_map/ppermute | solution.py:418
  17.8 8.1 %collective-permute-start.8 = (f32[4,2,8,512]{3,2,1,0:T(8,128)S(1)}, f32[4,2,8,512]{3,2,1,0:T(8,128)S(1)}, u32[]{:S(2)}, u32[]{:S(2)}) collective-permute-start(f32[4,2,8,512]{3,2,1,0:T(8,128)S(1)} %collective-permute-done.4.second), channel_id=1, source_target_pairs={{0,8},{8,0},{16,24},{24,16},{1,9},{9,1},{17,25},{25,17},{2,10},{10... | collective-permute-start | bytes 393224 | tf_op jit(solution)/shard_map/ppermute | solution.py:418
  20.3 5.6 %collective-permute-start.7 = (f32[4,2,8,512]{3,2,1,0:T(8,128)S(1)}, f32[4,2,8,512]{3,2,1,0:T(8,128)S(1)}, u32[]{:S(2)}, u32[]{:S(2)}) collective-permute-start(f32[4,2,8,512]{3,2,1,0:T(8,128)S(1)} %collective-permute-done.3.second), channel_id=1, source_target_pairs={{0,16},{8,24},{16,0},{24,8},{1,17},{9,25},{17,1},{25,9},{2,18},{10... | collective-permute-start | bytes 393224 | tf_op jit(solution)/shard_map/ppermute | solution.py:418
  21.9 5.6 %copy-start = (bf16[256,384]{1,0:T(8,128)(2,1)S(1)}, bf16[256,384]{1,0:T(8,128)(2,1)}, u32[]{:S(2)}) copy-start(bf16[256,384]{1,0:T(8,128)(2,1)} %constant.8.clone.refs_12_) | copy-start | bytes 589828
  21.9 5.6 %copy-start.1 = (bf16[384,192]{1,0:T(8,128)(2,1)S(1)}, bf16[384,192]{1,0:T(8,128)(2,1)}, u32[]{:S(2)}) copy-start(bf16[384,192]{1,0:T(8,128)(2,1)} %constant.7.clone.refs_11_) | copy-start | bytes 442372
  21.9 5.6 %copy-start.2 = (f32[128,128]{1,0:T(8,128)S(1)}, f32[128,128]{1,0:T(8,128)}, u32[]{:S(2)}) copy-start(f32[128,128]{1,0:T(8,128)} %constant.6.clone.refs_10_) | copy-start | bytes 196612
  21.9 5.5 %collective-permute-start.11 = (f32[2,4,2,8,512]{4,3,2,1,0:T(8,128)S(1)}, f32[2,4,2,8,512]{4,3,2,1,0:T(8,128)S(1)}, u32[]{:S(2)}, u32[]{:S(2)}) collective-permute-start(f32[2,4,2,8,512]{4,3,2,1,0:T(8,128)S(1)} %shard_map.79.refs_2_), channel_id=1, source_target_pairs={{0,1},{1,0},{2,3},{3,2},{4,5},{5,4},{6,7},{7,6},{8,9},{9,8},{10,11... | collective-permute-start | bytes 786440 | tf_op jit(solution)/shard_map/ppermute | solution.py:418
  22.0 5.4 %collective-permute-start.9 = (f32[2,4,2,8,512]{4,3,2,1,0:T(8,128)S(1)}, f32[2,4,2,8,512]{4,3,2,1,0:T(8,128)S(1)}, u32[]{:S(2)}, u32[]{:S(2)}) collective-permute-start(f32[2,4,2,8,512]{4,3,2,1,0:T(8,128)S(1)} %shard_map.77.refs_0_), channel_id=1, source_target_pairs={{0,1},{1,0},{2,3},{3,2},{4,5},{5,4},{6,7},{7,6},{8,9},{9,8},{10,11... | collective-permute-start | bytes 786440 | tf_op jit(solution)/shard_map/ppermute | solution.py:418
  25.9 1.3 %collective-permute-start.12 = (f32[4,2,8,512]{3,2,1,0:T(8,128)S(1)}, f32[4,2,8,512]{3,2,1,0:T(8,128)S(1)}, u32[]{:S(2)}, u32[]{:S(2)}) collective-permute-start(f32[4,2,8,512]{3,2,1,0:T(8,128)S(1)} %collective-permute-done.7.refs_3_), channel_id=1, source_target_pairs={{0,1},{1,0},{2,3},{3,2},{4,5},{5,4},{6,7},{7,6},{8,9},{9,8},{10,11... | collective-permute-start | bytes 393224 | tf_op jit(solution)/shard_map/ppermute | solution.py:418
  25.9 1.5 %collective-permute-start.13 = (f32[4,2,8,512]{3,2,1,0:T(8,128)S(1)}, f32[4,2,8,512]{3,2,1,0:T(8,128)S(1)}, u32[]{:S(2)}, u32[]{:S(2)}) collective-permute-start(f32[4,2,8,512]{3,2,1,0:T(8,128)S(1)} %collective-permute-done.8.refs_4_), channel_id=1, source_target_pairs={{0,1},{1,0},{2,3},{3,2},{4,5},{5,4},{6,7},{7,6},{8,9},{9,8},{10,11... | collective-permute-start | bytes 393224 | tf_op jit(solution)/shard_map/ppermute | solution.py:418
